TPU v7x, 32 devices: a whole 2x2x4 slice. The times are simulated.
32 devices in a mesh: grp: 2 (over y), gx: 4 (over z), gy: 4 (over x, core).
Axes of the slice: x: 2, y: 2, z: 4, core: 2. Of those that a mesh axis runs over, the one named last changes fastest.
Arguments:
- source: bfloat16 [512, 256, 128], P(('grp', 'gx'), 'gy'), parts along dimension 0, may hold values from -6 to 6
- field: bfloat16 [512, 256, 128], P(('grp', 'gx'), 'gy'), parts along dimension 0, may hold values from -3 to 3
- kerr: float32 [512, 256], P(('grp', 'gx'), 'gy'), parts along dimension 0, may hold values from 0.05 to 0.3
- wave: float32 [512, 256], P(('grp', 'gx'), 'gy'), parts along dimension 0, may hold values from 0.5 to 2
- leaf_ops: bfloat16 [16, 16, 256, 256], P('gx', 'gy'), may hold values from -0.375 to 0.375
- transfer_ops: float32 [4, 256, 64], P('gx', 'gy'), may hold values from 0 to 1
Outputs:
- updated: bfloat16 [512, 256, 128], P(('grp', 'gx'), 'gy'), parts along dimension 0
- residual: bfloat16 [512, 256, 128], P(('grp', 'gx'), 'gy'), parts along dimension 0
There are 2 independent parts, one for each index of `grp`. A program takes and returns all parts, laid end to end along the dimension named above; an argument that names none is the same for every part. Nothing has to cross between parts.
All inputs are finite; a program needn't handle non-finite values.
Results may differ from a plain program's by a relative error of at most 0.015.
Values may be sent and summed in bfloat16 or wider, within the bound.
A program may use at most 64 MiB of HBM per device.

v0:
```python
import jax
import jax.numpy as jnp
from jax import lax
from jax.sharding import PartitionSpec as P

lift_weight = 0.3


def entering(part, axis, combine, identity, reverse):
    count = lax.axis_size(axis)
    place = lax.axis_index(axis)
    ahead = count - 1 - place if reverse else place
    gathered = jax.tree.map(lambda a: lax.all_gather(a, axis), part)
    state = jax.tree.map(lambda a, e: jnp.zeros_like(a) + jnp.asarray(e, a.dtype), part, identity)

    def one(hop, state):
        source = count - 1 - hop if reverse else hop
        return combine(
            state, jax.tree.map(lambda a: lax.dynamic_index_in_dim(a, source, 0, False), gathered)
        )

    return lax.fori_loop(0, ahead, one, state)


def with_halo(block, sides, width):
    for axis, dim in sides:
        count = lax.axis_size(axis)
        forward = [(i, i + 1) for i in range(count - 1)]
        backward = [(target, source) for source, target in forward]
        low = lax.ppermute(
            lax.slice_in_dim(block, block.shape[dim] - width, None, axis=dim), axis, forward
        )
        high = lax.ppermute(lax.slice_in_dim(block, 0, width, axis=dim), axis, backward)
        block = jnp.concatenate([low, block, high], axis=dim)
    return block


def product(left, right):
    return jnp.dot(left, right, precision=lax.Precision.HIGHEST)


def compose(earlier, later):
    return (product(later[0], earlier[0]), product(later[0], earlier[1]) + later[1])


def per_device(source, field, kerr, wave, leaf_ops, transfer_ops):
    x_points, y_points, columns = source.shape
    leaves_x, leaves_y, leaf_pts, _ = leaf_ops.shape
    points = x_points // leaves_x
    source_f = source.astype(jnp.float32)
    field_f = field.astype(jnp.float32)
    kerr_source = (source_f - kerr[:, :, None] * field_f * field_f * field_f).astype(jnp.bfloat16)
    leaves = (
        kerr_source.reshape(leaves_x, points, leaves_y, points, columns)
        .transpose(0, 2, 1, 3, 4)
        .reshape(leaves_x, leaves_y, leaf_pts, columns)
    )
    solved = jnp.einsum("abpq,abqn->abpn", leaf_ops, leaves, preferred_element_type=jnp.float32)
    particular_solution = (
        solved.reshape(leaves_x, leaves_y, points, points, columns)
        .transpose(0, 2, 1, 3, 4)
        .reshape(x_points, y_points, columns)
    )
    right_face = particular_solution[-1]
    left_face = particular_solution[0]
    own_map = transfer_ops[0]
    ident = (jnp.eye(y_points, dtype=jnp.float32), jnp.zeros((y_points, columns), jnp.float32))
    _, w_in = entering((own_map, right_face), "gx", compose, ident, False)
    _, z_in = entering((own_map.T, left_face), "gx", compose, ident, True)
    offsets = jnp.arange(x_points).astype(jnp.float32)
    left_prof = ((x_points - offsets) / x_points)[:, None, None]
    right_prof = ((offsets + 1.0) / x_points)[:, None, None]
    updated = (
        particular_solution + lift_weight * (left_prof * w_in[None] + right_prof * z_in[None])
    ).astype(jnp.bfloat16)
    padded_patches = with_halo(updated, (("gx", 0), ("gy", 1)), 1).astype(jnp.float32)
    values = updated.astype(jnp.float32)
    laplacian_operator = (
        padded_patches[2:, 1:-1]
        + padded_patches[:-2, 1:-1]
        + padded_patches[1:-1, 2:]
        + padded_patches[1:-1, :-2]
        - 4.0 * values
    )
    residual = (
        laplacian_operator
        + wave[:, :, None] * values
        + kerr[:, :, None] * values * values * values
        - source_f
    )
    return (updated, residual.astype(jnp.bfloat16))


def solution(mesh):
    return jax.shard_map(
        per_device,
        mesh=mesh,
        in_specs=(
            P(("grp", "gx"), "gy", None),
            P(("grp", "gx"), "gy", None),
            P(("grp", "gx"), "gy"),
            P(("grp", "gx"), "gy"),
            P("gx", "gy", None, None),
            P("gx", "gy", None),
        ),
        out_specs=(P(("grp", "gx"), "gy", None), P(("grp", "gx"), "gy", None)),
        check_vma=False,
    )
```

profile of v0, /device:TPU:1, one launch (start us, length us, event | category | flops | bytes accessed | tf_op | source)
XLA Modules:
  0.0 92.6 jit_solution(15015385495708423856)
XLA Ops:
  0.6 0.0 copy-start
  0.7 1.0 %copy.23 = f32[1,64,64]{1,2,0:T(8,128)S(1)} copy(f32[1,64,64]{2,1,0:T(8,128)} %param.15) | data formatting | bytes 32768 | tf_op args[5]
  1.6 12.3 %all_gather.15 = f32[4,64,64]{2,1,0:T(8,128)S(1)} all-gather(f32[1,64,64]{2,1,0:T(8,128)} %param.15), channel_id=1, replica_groups=mesh['grp'=2,'gx'=4,'gy'=4] {'gx'}, dimensions={0}, use_global_device_ids=true | all-gather | bytes 81920 | tf_op jit(solution)/shard_map/all_gather | solution.py:13
  14.0 10.5 %all-gather = f32[256,64]{1,0:T(8,128)S(1)} all-gather(f32[64,64]{1,0:T(8,128)S(1)} %bitcast.47), channel_id=2, replica_groups=mesh['grp'=2,'gx'=4,'gy'=4] {'gx'}, dimensions={0}, use_global_device_ids=true | all-gather | bytes 81920 | tf_op jit(solution)/shard_map/all_gather | solution.py:13
  24.5 1.9 %fusion.6 = bf16[64,64,128]{2,1,0:T(8,128)(2,1)S(1)} fusion(bf16[64,64,128]{2,1,0:T(8,128)(2,1)} %param.10, bf16[64,64,128]{2,1,0:T(8,128)(2,1)} %param.11, f32[64,64]{1,0:T(8,128)} %param.12), kind=kLoop, calls=%fused_computation.16 | loop fusion | flops 3670016 | bytes 3162112 | tf_op jit(solution)/shard_map/convert_element_type | solution.py:52
  26.4 0.3 copy.19
  26.7 2.2 %convolution_bitcast_fusion = f32[4,4,256,128]{2,3,1,0:T(8,128)} fusion(bf16[4,4,256,128]{3,2,1,0:T(8,128)(2,1)S(1)} %bitcast.44, bf16[4,4,256,256]{3,2,1,0:T(8,128)(2,1)S(1)} %copy-done), kind=kOutput, calls=%fused_computation.25 | convolution fusion | flops 268435456 | bytes 5242880 | tf_op jit(solution)/shard_map/abpq,abqn->abpn/dot_general | solution.py:58
  28.9 2.9 %copy.21 = f32[4,4,256,128]{3,2,1,0:T(8,128)} copy(f32[4,4,256,128]{2,3,1,0:T(8,128)} %convolution_bitcast_fusion) | data formatting | bytes 4194304 | tf_op jit(solution)/shard_map/abpq,abqn->abpn/dot_general | solution.py:58
  31.8 1.8 %copy.22 = f32[4,16,4,16,128]{4,3,2,1,0:T(8,128)S(1)} copy(f32[4,16,4,16,128]{4,3,1,2,0:T(8,128)} %bitcast.43) | data formatting | bytes 4194304 | tf_op jit(solution)/shard_map/transpose | solution.py:61
  33.6 1.3 %copy-done.1 = f32[4,16,4,16,128]{4,3,2,1,0:T(8,128)} copy-done((f32[4,16,4,16,128]{4,3,2,1,0:T(8,128)}, f32[4,16,4,16,128]{4,3,2,1,0:T(8,128)S(1)}, u32[]{:S(2)}) %copy-start.1) | copy-done | bytes 2097176
  35.0 10.5 %all_gather.16 = f32[4,64,128]{2,1,0:T(8,128)S(1)} all-gather(f32[1,64,128]{2,1,0:T(8,128)S(1)} %get-tuple-element.152), channel_id=1, replica_groups=mesh['grp'=2,'gx'=4,'gy'=4] {'gx'}, dimensions={0}, use_global_device_ids=true | all-gather | bytes 163840 | tf_op jit(solution)/shard_map/all_gather | solution.py:13
  45.4 10.8 %all_gather.19 = f32[4,64,128]{2,1,0:T(8,128)S(1)} all-gather(f32[1,64,128]{2,1,0:T(8,128)S(1)} %get-tuple-element.153), channel_id=1, replica_groups=mesh['grp'=2,'gx'=4,'gy'=4] {'gx'}, dimensions={0}, use_global_device_ids=true | all-gather | bytes 163840 | tf_op jit(solution)/shard_map/all_gather | solution.py:13
  56.3 0.6 while.27
  56.3 0.2 convolution_add_fusion.5
  56.5 0.2 convolution_add_fusion.5
  56.7 0.2 convolution_add_fusion.5
  56.9 2.1 %add_convert_fusion = bf16[64,64,128]{2,1,0:T(8,128)(2,1)S(1)} fusion(f32[64,64,128]{2,1,0:T(8,128)} %bitcast.41, f32[64,128]{1,0:T(8,128)S(1)} %get-tuple-element.131, f32[64]{0:T(128)S(1)} %get-tuple-element.158, f32[64,128]{1,0:T(8,128)S(1)} %get-tuple-element.130, f32[64]{0:T(128)S(1)} %get-tuple-element.159), kind=kLoop, calls=%fused_computation.24 | loop fusion | flops 3145728 | bytes 3211776 | tf_op jit(solution)/shard_map/convert_element_type | solution.py:75
  59.0 0.0 copy-start.3
  59.0 3.1 %collective-permute-start = (bf16[1,64,128]{2,1,0:T(8,128)(2,1)S(1)}, bf16[1,64,128]{2,1,0:T(8,128)(2,1)S(1)}, u32[]{:S(2)}, u32[]{:S(2)}) collective-permute-start(bf16[1,64,128]{2,1,0:T(8,128)(2,1)S(1)} %get-tuple-element.156), channel_id=1, source_target_pairs={{0,4},{4,8},{8,12},{1,5},{5,9},{9,13},{2,6},{6,10},{10,14},{3,7},{... | collective-permute-start | bytes 49160 | tf_op jit(solution)/shard_map/ppermute | solution.py:30
  62.2 0.0 copy-start.4
  62.2 0.0 copy-start.5
  62.2 0.0 copy-start.6
  62.2 1.6 %collective-permute-start.1 = (bf16[1,64,128]{2,1,0:T(8,128)(2,1)S(1)}, bf16[1,64,128]{2,1,0:T(8,128)(2,1)S(1)}, u32[]{:S(2)}, u32[]{:S(2)}) collective-permute-start(bf16[1,64,128]{2,1,0:T(8,128)(2,1)S(1)} %get-tuple-element.157), channel_id=1, source_target_pairs={{4,0},{8,4},{12,8},{5,1},{9,5},{13,9},{6,2},{10,6},{14,10},{7,3},{... | collective-permute-start | bytes 49160 | tf_op jit(solution)/shard_map/ppermute | solution.py:33
  63.8 0.0 collective-permute-done
  63.8 3.5 %collective-permute-done.1 = bf16[1,64,128]{2,1,0:T(8,128)(2,1)S(1)} collective-permute-done((bf16[1,64,128]{2,1,0:T(8,128)(2,1)S(1)}, bf16[1,64,128]{2,1,0:T(8,128)(2,1)S(1)}, u32[]{:S(2)}, u32[]{:S(2)}) %collective-permute-start.1) | collective-permute-done | bytes 16416 | tf_op jit(solution)/shard_map/ppermute | solution.py:33
  67.2 0.1 pad_maximum_fusion.2
  67.3 16.3 %collective-permute-start.2 = (bf16[66,1,128]{2,1,0:T(2,128)(2,1)S(1)}, bf16[66,1,128]{2,1,0:T(2,128)(2,1)S(1)}, u32[]{:S(2)}, u32[]{:S(2)}) collective-permute-start(bf16[66,1,128]{2,1,0:T(2,128)(2,1)S(1)} %get-tuple-element.154), channel_id=1, source_target_pairs={{0,1},{1,2},{2,3},{4,5},{5,6},{6,7},{8,9},{9,10},{10,11},{12,13},{... | collective-permute-start | bytes 50696 | tf_op jit(solution)/shard_map/ppermute | solution.py:30
  83.6 1.9 %collective-permute-start.3 = (bf16[66,1,128]{2,1,0:T(2,128)(2,1)S(1)}, bf16[66,1,128]{2,1,0:T(2,128)(2,1)S(1)}, u32[]{:S(2)}, u32[]{:S(2)}) collective-permute-start(bf16[66,1,128]{2,1,0:T(2,128)(2,1)S(1)} %get-tuple-element.155), channel_id=1, source_target_pairs={{1,0},{2,1},{3,2},{5,4},{6,5},{7,6},{9,8},{10,9},{11,10},{13,12},{... | collective-permute-start | bytes 50696 | tf_op jit(solution)/shard_map/ppermute | solution.py:33
  85.6 0.0 collective-permute-done.2
  85.6 3.3 %collective-permute-done.3 = bf16[66,1,128]{2,1,0:T(2,128)(2,1)S(1)} collective-permute-done((bf16[66,1,128]{2,1,0:T(2,128)(2,1)S(1)}, bf16[66,1,128]{2,1,0:T(2,128)(2,1)S(1)}, u32[]{:S(2)}, u32[]{:S(2)}) %collective-permute-start.3) | collective-permute-done | bytes 16928 | tf_op jit(solution)/shard_map/ppermute | solution.py:33
  88.9 0.5 maximum_convert_fusion
  89.4 3.2 %fusion.7 = bf16[64,64,128]{2,1,0:T(8,128)(2,1)} fusion(bf16[64,64,128]{2,1,0:T(8,128)(2,1)S(1)} %copy-done.4, f32[66,66,128]{2,1,0:T(8,128)S(1)} %maximum_convert_fusion, f32[64,64]{1,0:T(8,128)S(1)} %copy-done.6, f32[64,64]{1,0:T(8,128)S(1)} %copy-done.5, f32[64,64,128]{2,1,0:T(8,128)S(1)} %bitcast.42, f32[64,128]{1,0:T(8,128)S(1)} %get-tuple-element.131, ...), kind=kLoop, calls=%fused_computation.17 | loop fusion | flops 11010048 | bytes 12681728 | tf_op jit(solution)/shard_map/convert_element_type | solution.py:91
  (17 shorter events, 0.1 us)
Async XLA Ops:
  0.6 26.1 %copy-start = (bf16[4,4,256,256]{3,2,1,0:T(8,128)(2,1)S(1)}, bf16[4,4,256,256]{3,2,1,0:T(8,128)(2,1)}, u32[]{:S(2)}) copy-start(bf16[4,4,256,256]{3,2,1,0:T(8,128)(2,1)} %param.14) | copy-start | bytes 6291460
  33.6 1.3 %copy-start.1 = (f32[4,16,4,16,128]{4,3,2,1,0:T(8,128)}, f32[4,16,4,16,128]{4,3,2,1,0:T(8,128)S(1)}, u32[]{:S(2)}) copy-start(f32[4,16,4,16,128]{4,3,2,1,0:T(8,128)S(1)} %copy.22) | copy-start | bytes 6291460
  59.0 30.4 %copy-start.3 = (bf16[64,64,128]{2,1,0:T(8,128)(2,1)}, bf16[64,64,128]{2,1,0:T(8,128)(2,1)S(1)}, u32[]{:S(2)}) copy-start(bf16[64,64,128]{2,1,0:T(8,128)(2,1)S(1)} %add_convert_fusion) | copy-start | bytes 3145732
  59.0 4.8 %collective-permute-start = (bf16[1,64,128]{2,1,0:T(8,128)(2,1)S(1)}, bf16[1,64,128]{2,1,0:T(8,128)(2,1)S(1)}, u32[]{:S(2)}, u32[]{:S(2)}) collective-permute-start(bf16[1,64,128]{2,1,0:T(8,128)(2,1)S(1)} %get-tuple-element.156), channel_id=1, source_target_pairs={{0,4},{4,8},{8,12},{1,5},{5,9},{9,13},{2,6},{6,10},{10,14},{3,7},{... | collective-permute-start | bytes 49160 | tf_op jit(solution)/shard_map/ppermute | solution.py:30
  62.2 27.2 %copy-start.2 = (f32[4,16,4,16,128]{4,3,2,1,0:T(8,128)S(1)}, f32[4,16,4,16,128]{4,3,2,1,0:T(8,128)}, u32[]{:S(2)}) copy-start(f32[4,16,4,16,128]{4,3,2,1,0:T(8,128)} %copy-done.1) | copy-start | bytes 6291460
  62.2 27.2 %copy-start.4 = (bf16[64,64,128]{2,1,0:T(8,128)(2,1)S(1)}, bf16[64,64,128]{2,1,0:T(8,128)(2,1)}, u32[]{:S(2)}) copy-start(bf16[64,64,128]{2,1,0:T(8,128)(2,1)} %param.10) | copy-start | bytes 3145732
  62.2 27.2 %copy-start.5 = (f32[64,64]{1,0:T(8,128)S(1)}, f32[64,64]{1,0:T(8,128)}, u32[]{:S(2)}) copy-start(f32[64,64]{1,0:T(8,128)} %param.12) | copy-start | bytes 49156
  62.2 27.2 %copy-start.6 = (f32[64,64]{1,0:T(8,128)S(1)}, f32[64,64]{1,0:T(8,128)}, u32[]{:S(2)}) copy-start(f32[64,64]{1,0:T(8,128)} %param.13) | copy-start | bytes 49156
  62.2 5.0 %collective-permute-start.1 = (bf16[1,64,128]{2,1,0:T(8,128)(2,1)S(1)}, bf16[1,64,128]{2,1,0:T(8,128)(2,1)S(1)}, u32[]{:S(2)}, u32[]{:S(2)}) collective-permute-start(bf16[1,64,128]{2,1,0:T(8,128)(2,1)S(1)} %get-tuple-element.157), channel_id=1, source_target_pairs={{4,0},{8,4},{12,8},{5,1},{9,5},{13,9},{6,2},{10,6},{14,10},{7,3},{... | collective-permute-start | bytes 49160 | tf_op jit(solution)/shard_map/ppermute | solution.py:33
  67.3 18.3 %collective-permute-start.2 = (bf16[66,1,128]{2,1,0:T(2,128)(2,1)S(1)}, bf16[66,1,128]{2,1,0:T(2,128)(2,1)S(1)}, u32[]{:S(2)}, u32[]{:S(2)}) collective-permute-start(bf16[66,1,128]{2,1,0:T(2,128)(2,1)S(1)} %get-tuple-element.154), channel_id=1, source_target_pairs={{0,1},{1,2},{2,3},{4,5},{5,6},{6,7},{8,9},{9,10},{10,11},{12,13},{... | collective-permute-start | bytes 50696 | tf_op jit(solution)/shard_map/ppermute | solution.py:30
  83.6 5.2 %collective-permute-start.3 = (bf16[66,1,128]{2,1,0:T(2,128)(2,1)S(1)}, bf16[66,1,128]{2,1,0:T(2,128)(2,1)S(1)}, u32[]{:S(2)}, u32[]{:S(2)}) collective-permute-start(bf16[66,1,128]{2,1,0:T(2,128)(2,1)S(1)} %get-tuple-element.155), channel_id=1, source_target_pairs={{1,0},{2,1},{3,2},{5,4},{6,5},{7,6},{9,8},{10,9},{11,10},{13,12},{... | collective-permute-start | bytes 50696 | tf_op jit(solution)/shard_map/ppermute | solution.py:33
where the time goes:
time: 93 us; the launch traced here: 92.6 us
  blocking collectives  44.1 us (47%)
  starting transfers between devices  22.9 us (25%)
  other arithmetic  7.78 us (8%)
  local copies, waits for them, and re-layouts  7.37 us (8%)
  waiting for transfers between devices  6.78 us (7%)
  matrix products  2.68 us (3%)
    all_gather x4, blocking collectives, entering(): gathered = jax.tree.map(lambda a: lax.all_gather(a, axis), part)  44.1 us
    ppermute x2, starting transfers between devices, with_halo(): lax.ppermute(lax.slice_in_dim(block, block.shape[dim] - width, None, axis...  19.5 us
    ppermute x2, waiting for transfers between devices, with_halo(): lax.ppermute(lax.slice_in_dim(block, 0, width, axis=dim), axis, backward)  6.77 us
    ppermute x2, starting transfers between devices, with_halo(): lax.ppermute(lax.slice_in_dim(block, 0, width, axis=dim), axis, backward)  3.48 us
    convert_element_type x1, other arithmetic, per_device(): return (updated, residual.astype(jnp.bfloat16))  3.22 us
    dot_general x1, local copies, waits for them, and re-layouts, per_device(): jnp.einsum('abpq,abqn->abpn', leaf_ops, leaves, preferred_element_type=jn...  2.92 us
    unnamed x15, local copies, waits for them, and re-layouts  2.34 us
    dot_general x1, matrix products, per_device(): jnp.einsum('abpq,abqn->abpn', leaf_ops, leaves, preferred_element_type=jn...  2.18 us
  transfers between devices with their start and end apart: 4, of which 2 were waited for; matrix products, arithmetic and copies ran while one was open for 0% of the time, Pallas kernels for 0%

commit v1 on v0

v1 whole, which is shorter than its diff:
```python
import functools

import jax
import jax.numpy as jnp
from jax import lax
from jax.experimental import pallas as pl
from jax.experimental.pallas import tpu as pltpu
from jax.sharding import PartitionSpec as P

lift_weight = 0.3
MESH = pl.DeviceIdType.MESH
F32 = jnp.float32
BF16 = jnp.bfloat16
PAD = 8


def kernel(
    n_gx, n_gy,
    source, field, kerr, wave, leaf_ops, transfer_ops,
    updated, residual,
    src_v, fld_v, kerr_v, wave_v, map_v, ops_v, edge_ops, leaf_src, grid, kerr_b, wave_b,
    upd_v, res_v, face_out, face_in, op_out, op_in, edge_out, edge_in,
    row_sems, small_sems, ops_sems, edge_sems, out_sems,
    face_send, face_recv, op_send, op_recv, halo_send, halo_recv,
):
    x_points, y_points, columns = src_v.shape
    leaves_x, leaves_y, leaf_pts, _ = ops_v.shape
    q = x_points // leaves_x
    half = y_points // 2
    last = leaves_x - 1
    me = lax.axis_index("gx")
    col = lax.axis_index("gy")

    small = [
        pltpu.make_async_copy(kerr, kerr_v, small_sems.at[0]),
        pltpu.make_async_copy(wave, wave_v, small_sems.at[1]),
        pltpu.make_async_copy(transfer_ops.at[0], map_v, small_sems.at[2]),
    ]
    for c in small:
        c.start()
    order = [0, last] + list(range(1, last))
    rows, edges, ops = {}, [], {}
    for a in order:
        span = pl.ds(a * q, q)
        rows[a] = (
            pltpu.make_async_copy(source.at[span], src_v.at[span], row_sems.at[0, a]),
            pltpu.make_async_copy(field.at[span], fld_v.at[span], row_sems.at[1, a]),
        )
    for i, (a, first) in enumerate(((0, 0), (last, leaf_pts - q))):
        edges.append(
            pltpu.make_async_copy(
                leaf_ops.at[a, :, pl.ds(first, q), :], edge_ops.at[i], edge_sems.at[i]
            )
        )
    for a in order:
        ops[a] = pltpu.make_async_copy(leaf_ops.at[a], ops_v.at[a], ops_sems.at[a])
    for a in order[:2]:
        rows[a][0].start()
        rows[a][1].start()
    for c in edges:
        c.start()
    for a in order[2:]:
        rows[a][0].start()
        rows[a][1].start()
    for a in order:
        ops[a].start()

    barrier = pltpu.get_barrier_semaphore()

    def greet(p, carry):
        @pl.when(p != me)
        def _():
            pl.semaphore_signal(barrier, inc=1, device_id={"gx": p}, device_id_type=MESH)

        return carry

    lax.fori_loop(0, n_gx, greet, 0)

    @pl.when(col > 0)
    def _():
        pl.semaphore_signal(barrier, inc=1, device_id={"gy": col - 1}, device_id_type=MESH)

    @pl.when(col < n_gy - 1)
    def _():
        pl.semaphore_signal(barrier, inc=1, device_id={"gy": col + 1}, device_id_type=MESH)

    partners = (n_gx - 1) + jnp.where(col > 0, 1, 0) + jnp.where(col < n_gy - 1, 1, 0)

    for c in small:
        c.wait()
    coeff = jnp.transpose(jnp.concatenate([kerr_v[...], wave_v[...]], axis=0))
    own = map_v[...]
    own_t = jnp.transpose(own)
    for i, m in enumerate((own, own_t)):
        op_out[i] = jnp.concatenate([m[:half], m[half:]], axis=1).astype(BF16)

    def face_copy(side, slot, p):
        return pltpu.make_async_remote_copy(
            src_ref=face_out.at[side],
            dst_ref=face_in.at[slot],
            send_sem=face_send.at[p],
            recv_sem=face_recv.at[slot],
            device_id={"gx": p},
            device_id_type=MESH,
        )

    def op_copy(side, slot, p):
        return pltpu.make_async_remote_copy(
            src_ref=op_out.at[side],
            dst_ref=op_in.at[slot],
            send_sem=op_send.at[p],
            recv_sem=op_recv.at[slot],
            device_id={"gx": p},
            device_id_type=MESH,
        )

    def run(low, high, body):
        def step(p, carry):
            body(p)
            return carry

        lax.fori_loop(low, high, step, 0)

    inner = jnp.logical_and(me > 0, me < n_gx - 1)
    pl.semaphore_wait(barrier, partners)

    @pl.when(inner)
    def _():
        run(me + 1, n_gx, lambda p: op_copy(0, me, p).start())
        run(0, me, lambda p: op_copy(1, me, p).start())

    def leaf_row(a):
        rows[a][0].wait()
        rows[a][1].wait()
        for i in range(q):
            x = a * q + i
            k = jnp.broadcast_to(coeff[:, x : x + 1], (y_points, columns))
            kerr_b[x] = k
            f = fld_v[x].astype(F32)
            s = (src_v[x].astype(F32) - k * f * f * f).astype(BF16)
            for b in range(leaves_y):
                leaf_src[a, b, i * q : (i + 1) * q, :] = s[b * q : (b + 1) * q]

    for i, a in enumerate((0, last)):
        if i == 0 or last > 0:
            leaf_row(a)
        edges[i].wait()
        for b in range(leaves_y):
            face_out[1 - i, b * q : (b + 1) * q, :] = jnp.dot(
                edge_ops[i, b], leaf_src[a, b], preferred_element_type=F32
            ).astype(BF16)
    run(me + 1, n_gx, lambda p: face_copy(0, me, p).start())
    run(0, me, lambda p: face_copy(1, me, p).start())

    for a in order[2:]:
        leaf_row(a)
    for a in order:
        ops[a].wait()
        for b in range(leaves_y):
            solved = jnp.dot(ops_v[a, b], leaf_src[a, b], preferred_element_type=F32)
            for i in range(q):
                grid[1 + a * q + i, PAD + b * q : PAD + (b + 1) * q, :] = solved[i * q : (i + 1) * q]
    for x in range(x_points):
        wave_b[x] = jnp.broadcast_to(
            coeff[:, x_points + x : x_points + x + 1] - 4.0, (y_points, columns)
        )
    zero_row = jnp.zeros((1, columns), F32)
    for x in range(x_points):
        grid[1 + x, PAD - 1 : PAD, :] = zero_row
        grid[1 + x, PAD + y_points : PAD + y_points + 1, :] = zero_row
    low_edge = jnp.concatenate([grid[1 + x, PAD : PAD + 1, :] for x in range(x_points)], axis=0)
    high_edge = jnp.concatenate(
        [grid[1 + x, PAD + y_points - 1 : PAD + y_points, :] for x in range(x_points)], axis=0
    )

    def apply(packed, state):
        s = state.astype(BF16)
        z = jnp.zeros_like(s)
        wide = jnp.concatenate(
            [jnp.concatenate([s, z], axis=1), jnp.concatenate([z, s], axis=1)], axis=0
        )
        out = jnp.dot(packed, wide, preferred_element_type=F32)
        return jnp.concatenate([out[:, :columns], out[:, columns:]], axis=0)

    zeros = jnp.zeros((y_points, columns), F32)

    def arrived(s):
        face_copy(0, s, s).wait_recv()
        return face_in[s].astype(F32)

    def chain(begin, count, step):
        def first():
            return arrived(begin)

        state = lax.cond(count > 0, first, lambda: zeros)

        def hop(i, carry):
            _, now = carry
            s = begin + step * i
            op_copy(0, s, s).wait_recv()
            nxt = apply(op_in[s], now) + arrived(s)
            return now, nxt

        return lax.fori_loop(1, count, hop, (zeros, state))

    w_before, w = chain(0, me, 1)
    z_after, z = chain(n_gx - 1, n_gx - 1 - me, -1)
    w3, z3 = lift_weight * w, lift_weight * z

    position = lax.broadcasted_iota(jnp.int32, (x_points, columns), 0).astype(F32)
    left_prof = (x_points - position) / x_points
    right_prof = (position + 1.0) / x_points
    for i, (edge, y) in enumerate(((low_edge, 0), (high_edge, y_points - 1))):
        edge_out[i] = (
            edge + (left_prof * w3[y : y + 1, :] + right_prof * z3[y : y + 1, :])
        ).astype(BF16)

    def halo_copy(side, p):
        return pltpu.make_async_remote_copy(
            src_ref=edge_out.at[side],
            dst_ref=edge_in.at[1 - side],
            send_sem=halo_send.at[side],
            recv_sem=halo_recv.at[1 - side],
            device_id={"gy": p},
            device_id_type=MESH,
        )

    @pl.when(col > 0)
    def _():
        halo_copy(0, col - 1).start()

    @pl.when(col < n_gy - 1)
    def _():
        halo_copy(1, col + 1).start()

    tip = 1.0 / x_points
    body = pl.ds(PAD, y_points)

    @pl.when(me > 0)
    def _():
        face = face_in[jnp.maximum(me - 1, 0)].astype(F32)
        z_there = apply(op_out[1], z) + grid[1, body, :]
        there = face + lift_weight * (tip * w_before + z_there)
        grid[0, body, :] = there.astype(BF16).astype(F32)

    @pl.when(me == 0)
    def _():
        grid[0, body, :] = zeros

    @pl.when(me < n_gx - 1)
    def _():
        face = face_in[jnp.minimum(me + 1, n_gx - 1)].astype(F32)
        w_there = apply(op_out[0], w) + grid[x_points, body, :]
        there = face + lift_weight * (w_there + tip * z_after)
        grid[x_points + 1, body, :] = there.astype(BF16).astype(F32)

    @pl.when(me == n_gx - 1)
    def _():
        grid[x_points + 1, body, :] = zeros

    outs = []
    for a in range(leaves_x):

        def lift(i, carry):
            x = a * q + i
            at = lax.convert_element_type(x, F32)
            u = grid[1 + x, body, :] + (
                ((x_points - at) / x_points) * w3 + ((at + 1.0) / x_points) * z3
            )
            u = u.astype(BF16)
            upd_v[x] = u
            grid[1 + x, body, :] = u.astype(F32)
            return carry

        lax.fori_loop(0, q, lift, 0, unroll=4)
        span = pl.ds(a * q, q)
        outs.append(pltpu.make_async_copy(upd_v.at[span], updated.at[span], out_sems.at[a]))
        outs[-1].start()

    def finish(x, low, size):
        mid = grid[1 + x, PAD + low : PAD + low + size, :]
        near = (
            grid[x, PAD + low : PAD + low + size, :]
            + grid[2 + x, PAD + low : PAD + low + size, :]
        ) + (
            grid[1 + x, PAD + low - 1 : PAD + low + size - 1, :]
            + grid[1 + x, PAD + low + 1 : PAD + low + size + 1, :]
        )
        factor = wave_b[x, low : low + size, :] + kerr_b[x, low : low + size, :] * (mid * mid)
        res_v[x, low : low + size, :] = (
            near + (factor * mid - src_v[x, low : low + size, :].astype(F32))
        ).astype(BF16)

    def inside(x, carry):
        finish(x, q, y_points - 2 * q)
        return carry

    lax.fori_loop(0, x_points, inside, 0, unroll=4)
    part = pl.ds(q, y_points - 2 * q)
    outs.append(
        pltpu.make_async_copy(
            res_v.at[:, part, :], residual.at[:, part, :], out_sems.at[leaves_x]
        )
    )
    outs[-1].start()

    @pl.when(col > 0)
    def _():
        halo_copy(1, col - 1).wait_recv()
        got = edge_in[0].astype(F32)
        for x in range(x_points):
            grid[1 + x, PAD - 1 : PAD, :] = got[x : x + 1]

    @pl.when(col < n_gy - 1)
    def _():
        halo_copy(0, col + 1).wait_recv()
        got = edge_in[1].astype(F32)
        for x in range(x_points):
            grid[1 + x, PAD + y_points : PAD + y_points + 1, :] = got[x : x + 1]

    def sides(x, carry):
        finish(x, 0, q)
        finish(x, y_points - q, q)
        return carry

    lax.fori_loop(0, x_points, sides, 0, unroll=4)
    for i, low in enumerate((0, y_points - q)):
        part = pl.ds(low, q)
        outs.append(
            pltpu.make_async_copy(
                res_v.at[:, part, :], residual.at[:, part, :], out_sems.at[leaves_x + 1 + i]
            )
        )
        outs[-1].start()

    run(me + 1, n_gx, lambda p: face_copy(0, me, p).wait_send())
    run(0, me, lambda p: face_copy(1, me, p).wait_send())

    @pl.when(inner)
    def _():
        run(me + 1, n_gx, lambda p: op_copy(0, me, p).wait_send())
        run(0, me, lambda p: op_copy(1, me, p).wait_send())

    @pl.when(col > 0)
    def _():
        halo_copy(0, col - 1).wait_send()

    @pl.when(col < n_gy - 1)
    def _():
        halo_copy(1, col + 1).wait_send()

    for c in outs:
        c.wait()


def per_device(n_gx, n_gy, source, field, kerr, wave, leaf_ops, transfer_ops):
    x_points, y_points, columns = source.shape
    leaves_x, leaves_y, leaf_pts, _ = leaf_ops.shape
    q = x_points // leaves_x
    grid_shape = (x_points, y_points, columns)
    dma = pltpu.SemaphoreType.DMA
    anywhere = pl.BlockSpec(memory_space=pl.ANY)
    return pl.pallas_call(
        functools.partial(kernel, n_gx, n_gy),
        out_shape=[jax.ShapeDtypeStruct(grid_shape, BF16)] * 2,
        in_specs=[anywhere] * 6,
        out_specs=[anywhere] * 2,
        scratch_shapes=[
            pltpu.VMEM(grid_shape, BF16),
            pltpu.VMEM(grid_shape, BF16),
            pltpu.VMEM((x_points, y_points), F32),
            pltpu.VMEM((x_points, y_points), F32),
            pltpu.VMEM((y_points, y_points), F32),
            pltpu.VMEM(leaf_ops.shape, BF16),
            pltpu.VMEM((2, leaves_y, q, leaf_pts), BF16),
            pltpu.VMEM((leaves_x, leaves_y, leaf_pts, columns), BF16),
            pltpu.VMEM((x_points + 2, y_points + 2 * PAD, columns), F32),
            pltpu.VMEM(grid_shape, F32),
            pltpu.VMEM(grid_shape, F32),
            pltpu.VMEM(grid_shape, BF16),
            pltpu.VMEM(grid_shape, BF16),
            pltpu.VMEM((2, y_points, columns), BF16),
            pltpu.VMEM((n_gx, y_points, columns), BF16),
            pltpu.VMEM((2, y_points // 2, 2 * y_points), BF16),
            pltpu.VMEM((n_gx, y_points // 2, 2 * y_points), BF16),
            pltpu.VMEM((2, x_points, columns), BF16),
            pltpu.VMEM((2, x_points, columns), BF16),
            dma((2, leaves_x)),
            dma((3,)),
            dma((leaves_x,)),
            dma((2,)),
            dma((leaves_x + 3,)),
            dma((n_gx,)),
            dma((n_gx,)),
            dma((n_gx,)),
            dma((n_gx,)),
            dma((2,)),
            dma((2,)),
        ],
        compiler_params=pltpu.CompilerParams(
            collective_id=0, has_side_effects=True, vmem_limit_bytes=40 * 1024 * 1024
        ),
        cost_estimate=pl.CostEstimate(
            flops=2 * leaf_ops.size * columns, bytes_accessed=6 << 20, transcendentals=0
        ),
        name="kerr_step",
    )(source, field, kerr, wave, leaf_ops, transfer_ops)


def solution(mesh):
    return jax.shard_map(
        functools.partial(per_device, mesh.shape["gx"], mesh.shape["gy"]),
        mesh=mesh,
        in_specs=(
            P(("grp", "gx"), "gy", None),
            P(("grp", "gx"), "gy", None),
            P(("grp", "gx"), "gy"),
            P(("grp", "gx"), "gy"),
            P("gx", "gy", None, None),
            P("gx", "gy", None),
        ),
        out_specs=(P(("grp", "gx"), "gy", None), P(("grp", "gx"), "gy", None)),
        check_vma=False,
    )
```

time: 93 us -> 21.9 us (0.24)
  blocking collectives: 44.1 us -> 0 us
  starting transfers between devices: 22.9 us -> 0 us
  Pallas kernels: 0 us -> 12.5 us
  other arithmetic: 7.78 us -> 0 us
  waiting for transfers between devices: 6.78 us -> 0 us
  matrix products: 2.68 us -> 0 us
    all_gather x4 -> x0, blocking collectives: 44.1 us -> none  [entering(): gathered = jax.tree.map(lambda a: lax.all_gather(a, axis), part)]
    ppermute x4 -> x0, starting transfers between devices: 22.9 us -> none  [the longest x2 19.5 us: with_halo(): lax.ppermute(lax.slice_in_dim(block, block.shape[dim] - width, None, axis...]
    pallas_call x0 -> x1, Pallas kernels: none -> 12.5 us  [per_device(): pl.pallas_call(functools.partial(kernel, n_gx, n_gy), out_shape=[jax.Shap...]
    convert_element_type x4 -> x0, other arithmetic: 7.72 us -> none  [the longest x1 3.22 us: per_device(): return (updated, residual.astype(jnp.bfloat16))]
    ppermute x4 -> x0, waiting for transfers between devices: 6.78 us -> none  [the longest x2 6.77 us: with_halo(): lax.ppermute(lax.slice_in_dim(block, 0, width, axis=dim), axis, backward)]
    unnamed x15 -> x14, local copies, waits for them, and re-layouts: 2.34 us -> 8.25 us
    dot_general x1 -> x0, local copies, waits for them, and re-layouts: 2.92 us -> none  [per_device(): jnp.einsum('abpq,abqn->abpn', leaf_ops, leaves, preferred_element_type=jn...]
    dot_general x4 -> x0, matrix products: 2.68 us -> none  [the longest x1 2.18 us: per_device(): jnp.einsum('abpq,abqn->abpn', leaf_ops, leaves, preferred_element_type=jn...]
  transfers between devices with their start and end apart: 4 -> 0, of which waited for: 2 -> 0; matrix products, arithmetic and copies ran while one was open for 0% -> 0% of each run, Pallas kernels for 0% -> 0%
where the time goes in v1:
time: 21.9 us; the launch traced here: 21.4 us
  Pallas kernels  12.5 us (57%)
  local copies, waits for them, and re-layouts  8.25 us (38%)
  between operations  0.65 us (3%)
    pallas_call x1, Pallas kernels, per_device(): pl.pallas_call(functools.partial(kernel, n_gx, n_gy), out_shape=[jax.Shap...  12.5 us
    unnamed x14, local copies, waits for them, and re-layouts  8.25 us

profile of v1, /device:TPU:1, one launch (start us, length us, event | category | flops | bytes accessed | tf_op | source)
XLA Modules:
  0.0 21.4 jit_solution(17208596867944624627)
XLA Ops:
  0.6 0.0 copy-start
  0.6 1.6 %copy-done = bf16[4,4,256,256]{3,2,1,0:T(8,128)(2,1)S(1)} copy-done((bf16[4,4,256,256]{3,2,1,0:T(8,128)(2,1)S(1)}, bf16[4,4,256,256]{3,2,1,0:T(8,128)(2,1)}, u32[]{:S(2)}) %copy-start) | copy-done | bytes 2097176
  2.2 0.0 copy-start.1
  2.2 1.2 %copy-done.1 = bf16[64,64,128]{2,1,0:T(8,128)(2,1)S(1)} copy-done((bf16[64,64,128]{2,1,0:T(8,128)(2,1)S(1)}, bf16[64,64,128]{2,1,0:T(8,128)(2,1)}, u32[]{:S(2)}) %copy-start.1) | copy-done | bytes 1048600
  3.4 0.0 copy-start.2
  3.5 1.2 %copy-done.2 = bf16[64,64,128]{2,1,0:T(8,128)(2,1)S(1)} copy-done((bf16[64,64,128]{2,1,0:T(8,128)(2,1)S(1)}, bf16[64,64,128]{2,1,0:T(8,128)(2,1)}, u32[]{:S(2)}) %copy-start.2) | copy-done | bytes 1048600
  4.7 0.0 copy-start.3
  4.7 0.8 %copy-done.3 = f32[64,64]{1,0:T(8,128)S(1)} copy-done((f32[64,64]{1,0:T(8,128)S(1)}, f32[64,64]{1,0:T(8,128)}, u32[]{:S(2)}) %copy-start.3) | copy-done | bytes 16408
  5.4 0.0 copy-start.4
  5.4 0.8 %copy-done.4 = f32[64,64]{1,0:T(8,128)S(1)} copy-done((f32[64,64]{1,0:T(8,128)S(1)}, f32[64,64]{1,0:T(8,128)}, u32[]{:S(2)}) %copy-start.4) | copy-done | bytes 16408
  6.2 0.0 copy-start.5
  6.2 0.8 %copy-done.5 = f32[1,64,64]{2,1,0:T(8,128)S(1)} copy-done((f32[1,64,64]{2,1,0:T(8,128)S(1)}, f32[1,64,64]{2,1,0:T(8,128)}, u32[]{:S(2)}) %copy-start.5) | copy-done | bytes 16408
  6.9 12.5 %kerr_step.1 = (bf16[64,64,128]{2,1,0:T(8,128)(2,1)S(1)}, bf16[64,64,128]{2,1,0:T(8,128)(2,1)S(1)}) custom-call(bf16[64,64,128]{2,1,0:T(8,128)(2,1)S(1)} %copy-done.1, bf16[64,64,128]{2,1,0:T(8,128)(2,1)S(1)} %copy-done.2, f32[64,64]{1,0:T(8,128)S(1)} %copy-done.3, f32[64,64]{1,0:T(8,128)S(1)} %copy-done.4, bf16[4,4,256,256]{3,2,1,0:T(8,128)(2,1)S(1)} %copy-done, ...), custom_call_target="tpu_custom_call" | custom-call | flops 268435456 | bytes 6291456 | tf_op jit(solution)/shard_map/kerr_step/pallas_call | solution.py:363
  19.5 1.0 %copy.10 = bf16[64,64,128]{2,1,0:T(8,128)(2,1)} copy(bf16[64,64,128]{2,1,0:T(8,128)(2,1)S(1)} %get-tuple-element.4) | data formatting | bytes 2097152
  20.5 1.0 %copy.11 = bf16[64,64,128]{2,1,0:T(8,128)(2,1)} copy(bf16[64,64,128]{2,1,0:T(8,128)(2,1)S(1)} %get-tuple-element.5) | data formatting | bytes 2097152
Async XLA Ops:
  0.6 1.6 %copy-start = (bf16[4,4,256,256]{3,2,1,0:T(8,128)(2,1)S(1)}, bf16[4,4,256,256]{3,2,1,0:T(8,128)(2,1)}, u32[]{:S(2)}) copy-start(bf16[4,4,256,256]{3,2,1,0:T(8,128)(2,1)} %leaf_ops.1) | copy-start | bytes 6291460
  2.2 1.2 %copy-start.1 = (bf16[64,64,128]{2,1,0:T(8,128)(2,1)S(1)}, bf16[64,64,128]{2,1,0:T(8,128)(2,1)}, u32[]{:S(2)}) copy-start(bf16[64,64,128]{2,1,0:T(8,128)(2,1)} %source.1) | copy-start | bytes 3145732
  3.4 1.2 %copy-start.2 = (bf16[64,64,128]{2,1,0:T(8,128)(2,1)S(1)}, bf16[64,64,128]{2,1,0:T(8,128)(2,1)}, u32[]{:S(2)}) copy-start(bf16[64,64,128]{2,1,0:T(8,128)(2,1)} %field.1) | copy-start | bytes 3145732
  4.7 0.8 %copy-start.3 = (f32[64,64]{1,0:T(8,128)S(1)}, f32[64,64]{1,0:T(8,128)}, u32[]{:S(2)}) copy-start(f32[64,64]{1,0:T(8,128)} %kerr.1) | copy-start | bytes 49156
  5.4 0.8 %copy-start.4 = (f32[64,64]{1,0:T(8,128)S(1)}, f32[64,64]{1,0:T(8,128)}, u32[]{:S(2)}) copy-start(f32[64,64]{1,0:T(8,128)} %wave.1) | copy-start | bytes 49156
  6.2 0.8 %copy-start.5 = (f32[1,64,64]{2,1,0:T(8,128)S(1)}, f32[1,64,64]{2,1,0:T(8,128)}, u32[]{:S(2)}) copy-start(f32[1,64,64]{2,1,0:T(8,128)} %transfer_ops.1) | copy-start | bytes 49156

commit v2 on v1

--- a/solution.py
+++ b/solution.py
@@ -17,10 +17,10 @@
 def kernel(
     n_gx, n_gy,
     source, field, kerr, wave, leaf_ops, transfer_ops,
-    updated, residual,
+    upd_v, res_v,
     src_v, fld_v, kerr_v, wave_v, map_v, ops_v, edge_ops, leaf_src, grid, kerr_b, wave_b,
-    upd_v, res_v, face_out, face_in, op_out, op_in, edge_out, edge_in,
-    row_sems, small_sems, ops_sems, edge_sems, out_sems,
+    rims, face_out, face_in, op_out, op_in, edge_out, edge_in,
+    row_sems, small_sems, ops_sems, edge_sems,
     face_send, face_recv, op_send, op_recv, halo_send, halo_recv,
 ):
     x_points, y_points, columns = src_v.shape
@@ -258,80 +258,50 @@
     def _():
         grid[x_points + 1, body, :] = zeros
 
-    outs = []
-    for a in range(leaves_x):
-
-        def lift(i, carry):
-            x = a * q + i
-            at = lax.convert_element_type(x, F32)
-            u = grid[1 + x, body, :] + (
-                ((x_points - at) / x_points) * w3 + ((at + 1.0) / x_points) * z3
-            )
-            u = u.astype(BF16)
-            upd_v[x] = u
-            grid[1 + x, body, :] = u.astype(F32)
-            return carry
-
-        lax.fori_loop(0, q, lift, 0, unroll=4)
-        span = pl.ds(a * q, q)
-        outs.append(pltpu.make_async_copy(upd_v.at[span], updated.at[span], out_sems.at[a]))
-        outs[-1].start()
-
-    def finish(x, low, size):
-        mid = grid[1 + x, PAD + low : PAD + low + size, :]
-        near = (
-            grid[x, PAD + low : PAD + low + size, :]
-            + grid[2 + x, PAD + low : PAD + low + size, :]
-        ) + (
-            grid[1 + x, PAD + low - 1 : PAD + low + size - 1, :]
-            + grid[1 + x, PAD + low + 1 : PAD + low + size + 1, :]
-        )
-        factor = wave_b[x, low : low + size, :] + kerr_b[x, low : low + size, :] * (mid * mid)
-        res_v[x, low : low + size, :] = (
-            near + (factor * mid - src_v[x, low : low + size, :].astype(F32))
-        ).astype(BF16)
-
-    def inside(x, carry):
-        finish(x, q, y_points - 2 * q)
+    def lift(x, carry):
+        at = lax.convert_element_type(x, F32)
+        u = grid[1 + x, body, :] + (
+            ((x_points - at) / x_points) * w3 + ((at + 1.0) / x_points) * z3
+        )
+        u = u.astype(BF16)
+        upd_v[x] = u
+        grid[1 + x, body, :] = u.astype(F32)
         return carry
 
-    lax.fori_loop(0, x_points, inside, 0, unroll=4)
-    part = pl.ds(q, y_points - 2 * q)
-    outs.append(
-        pltpu.make_async_copy(
-            res_v.at[:, part, :], residual.at[:, part, :], out_sems.at[leaves_x]
-        )
-    )
-    outs[-1].start()
+    lax.fori_loop(0, x_points, lift, 0, unroll=4)
+
+    def finish(x, carry):
+        mid = grid[1 + x, body, :]
+        near = (grid[x, body, :] + grid[2 + x, body, :]) + (
+            grid[1 + x, pl.ds(PAD - 1, y_points), :] + grid[1 + x, pl.ds(PAD + 1, y_points), :]
+        )
+        factor = wave_b[x] + kerr_b[x] * (mid * mid)
+        value = near + (factor * mid - src_v[x].astype(F32))
+        rims[0, pl.ds(x, 1), :] = value[:1]
+        rims[1, pl.ds(x, 1), :] = value[y_points - 1 :]
+        res_v[x] = value.astype(BF16)
+        return carry
+
+    lax.fori_loop(0, x_points, finish, 0, unroll=4)
+
+    row = lax.broadcasted_iota(jnp.int32, (q, columns), 0)
+
+    def amend(side, low, at):
+        full = rims[side] + edge_in[side].astype(F32)
+        for x in range(x_points):
+            tile = res_v[x, low : low + q, :].astype(F32)
+            new = jnp.where(row == at, full[x : x + 1], tile)
+            res_v[x, low : low + q, :] = new.astype(BF16)
 
     @pl.when(col > 0)
     def _():
         halo_copy(1, col - 1).wait_recv()
-        got = edge_in[0].astype(F32)
-        for x in range(x_points):
-            grid[1 + x, PAD - 1 : PAD, :] = got[x : x + 1]
+        amend(0, 0, 0)
 
     @pl.when(col < n_gy - 1)
     def _():
         halo_copy(0, col + 1).wait_recv()
-        got = edge_in[1].astype(F32)
-        for x in range(x_points):
-            grid[1 + x, PAD + y_points : PAD + y_points + 1, :] = got[x : x + 1]
-
-    def sides(x, carry):
-        finish(x, 0, q)
-        finish(x, y_points - q, q)
-        return carry
-
-    lax.fori_loop(0, x_points, sides, 0, unroll=4)
-    for i, low in enumerate((0, y_points - q)):
-        part = pl.ds(low, q)
-        outs.append(
-            pltpu.make_async_copy(
-                res_v.at[:, part, :], residual.at[:, part, :], out_sems.at[leaves_x + 1 + i]
-            )
-        )
-        outs[-1].start()
+        amend(1, y_points - q, q - 1)
 
     run(me + 1, n_gx, lambda p: face_copy(0, me, p).wait_send())
     run(0, me, lambda p: face_copy(1, me, p).wait_send())
@@ -349,7 +319,15 @@
     def _():
         halo_copy(1, col + 1).wait_send()
 
-    for c in outs:
+
+def store(upd_v, res_v, updated, residual, sems):
+    copies = [
+        pltpu.make_async_copy(upd_v, updated, sems.at[0]),
+        pltpu.make_async_copy(res_v, residual, sems.at[1]),
+    ]
+    for c in copies:
+        c.start()
+    for c in copies:
         c.wait()
 
 
@@ -359,12 +337,17 @@
     q = x_points // leaves_x
     grid_shape = (x_points, y_points, columns)
     dma = pltpu.SemaphoreType.DMA
-    anywhere = pl.BlockSpec(memory_space=pl.ANY)
-    return pl.pallas_call(
+    in_hbm = pl.BlockSpec(memory_space=pltpu.HBM)
+    in_vmem = pl.BlockSpec(memory_space=pltpu.VMEM)
+    operands = [
+        pltpu.with_memory_space_constraint(a, pltpu.HBM)
+        for a in (source, field, kerr, wave, leaf_ops, transfer_ops)
+    ]
+    results = pl.pallas_call(
         functools.partial(kernel, n_gx, n_gy),
-        out_shape=[jax.ShapeDtypeStruct(grid_shape, BF16)] * 2,
-        in_specs=[anywhere] * 6,
-        out_specs=[anywhere] * 2,
+        out_shape=[pltpu.VMEM(grid_shape, BF16)] * 2,
+        in_specs=[in_hbm] * 6,
+        out_specs=[in_vmem] * 2,
         scratch_shapes=[
             pltpu.VMEM(grid_shape, BF16),
             pltpu.VMEM(grid_shape, BF16),
@@ -377,8 +360,7 @@
             pltpu.VMEM((x_points + 2, y_points + 2 * PAD, columns), F32),
             pltpu.VMEM(grid_shape, F32),
             pltpu.VMEM(grid_shape, F32),
-            pltpu.VMEM(grid_shape, BF16),
-            pltpu.VMEM(grid_shape, BF16),
+            pltpu.VMEM((2, x_points, columns), F32),
             pltpu.VMEM((2, y_points, columns), BF16),
             pltpu.VMEM((n_gx, y_points, columns), BF16),
             pltpu.VMEM((2, y_points // 2, 2 * y_points), BF16),
@@ -389,7 +371,6 @@
             dma((3,)),
             dma((leaves_x,)),
             dma((2,)),
-            dma((leaves_x + 3,)),
             dma((n_gx,)),
             dma((n_gx,)),
             dma((n_gx,)),
@@ -404,7 +385,16 @@
             flops=2 * leaf_ops.size * columns, bytes_accessed=6 << 20, transcendentals=0
         ),
         name="kerr_step",
-    )(source, field, kerr, wave, leaf_ops, transfer_ops)
+    )(*operands)
+    return pl.pallas_call(
+        store,
+        out_shape=[pltpu.HBM(grid_shape, BF16)] * 2,
+        in_specs=[in_vmem] * 2,
+        out_specs=[in_hbm] * 2,
+        scratch_shapes=[dma((2,))],
+        cost_estimate=pl.CostEstimate(flops=0, bytes_accessed=4 << 20, transcendentals=0),
+        name="store_results",
+    )(*results)
 
 
 def solution(mesh):

time: 21.9 us -> 18.5 us (0.84); the launches traced: 21.4 us -> 18.3 us
  local copies, waits for them, and re-layouts: 8.25 us -> 1.98 us
  Pallas kernels: 12.5 us -> 15.7 us
    unnamed x14 -> x4, local copies, waits for them, and re-layouts: 8.25 us -> 1.98 us
    pallas_call x1 -> x2, Pallas kernels: 12.5 us -> 15.7 us  [the longest x1 12.8 us: per_device(): pl.pallas_call(functools.partial(kernel, n_gx, n_gy), out_shape=[pltpu.VM...]
where the time goes in v2:
time: 18.5 us; the launch traced here: 18.3 us
  Pallas kernels  15.7 us (85%)
  local copies, waits for them, and re-layouts  1.98 us (11%)
  between operations  0.65 us (4%)
    pallas_call x1, Pallas kernels, per_device(): pl.pallas_call(functools.partial(kernel, n_gx, n_gy), out_shape=[pltpu.VM...  12.8 us
    pallas_call x1, Pallas kernels, per_device(): pl.pallas_call(store, out_shape=[pltpu.HBM(grid_shape, BF16)] * 2, in_spe...  2.87 us
    unnamed x4, local copies, waits for them, and re-layouts  1.98 us

profile of v2, /device:TPU:1, one launch (start us, length us, event | category | flops | bytes accessed | tf_op | source)
XLA Modules:
  0.0 18.3 jit_solution(10001599081158428987)
XLA Ops:
  0.6 12.8 %kerr_step.1 = (bf16[64,64,128]{2,1,0:T(8,128)(2,1)S(1)}, bf16[64,64,128]{2,1,0:T(8,128)(2,1)S(1)}) custom-call(bf16[64,64,128]{2,1,0:T(8,128)(2,1)} %source.1, bf16[64,64,128]{2,1,0:T(8,128)(2,1)} %field.1, f32[64,64]{1,0:T(8,128)} %kerr.1, f32[64,64]{1,0:T(8,128)} %wave.1, bf16[4,4,256,256]{3,2,1,0:T(8,128)(2,1)} %leaf_ops.1, f32[1,64,64]{2,1,0:T(8,128)} %transfer_ops.1), custom_call_target="tpu_custom_call" | custom-call | flops 268435456 | bytes 6291456 | tf_op jit(solution)/shard_map/kerr_step/pallas_call | solution.py:346
  13.5 0.0 copy-start
  13.5 1.0 %copy-done = bf16[64,64,128]{2,1,0:T(8,128)(2,1)} copy-done((bf16[64,64,128]{2,1,0:T(8,128)(2,1)}, bf16[64,64,128]{2,1,0:T(8,128)(2,1)S(1)}, u32[]{:S(2)}) %copy-start) | copy-done | bytes 1048600
  14.4 0.0 copy-start.1
  14.4 1.0 %copy-done.1 = bf16[64,64,128]{2,1,0:T(8,128)(2,1)} copy-done((bf16[64,64,128]{2,1,0:T(8,128)(2,1)}, bf16[64,64,128]{2,1,0:T(8,128)(2,1)S(1)}, u32[]{:S(2)}) %copy-start.1) | copy-done | bytes 1048600
  15.5 2.9 %store_results.1 = (bf16[64,64,128]{2,1,0:T(8,128)(2,1)}, bf16[64,64,128]{2,1,0:T(8,128)(2,1)}) custom-call(bf16[64,64,128]{2,1,0:T(8,128)(2,1)} %copy-done, bf16[64,64,128]{2,1,0:T(8,128)(2,1)} %copy-done.1), custom_call_target="tpu_custom_call" | custom-call | bytes 4194304 | tf_op jit(solution)/shard_map/store_results/pallas_call | solution.py:389
Async XLA Ops:
  13.5 1.0 %copy-start = (bf16[64,64,128]{2,1,0:T(8,128)(2,1)}, bf16[64,64,128]{2,1,0:T(8,128)(2,1)S(1)}, u32[]{:S(2)}) copy-start(bf16[64,64,128]{2,1,0:T(8,128)(2,1)S(1)} %get-tuple-element.4.upd_v) | copy-start | bytes 3145732
  14.4 1.0 %copy-start.1 = (bf16[64,64,128]{2,1,0:T(8,128)(2,1)}, bf16[64,64,128]{2,1,0:T(8,128)(2,1)S(1)}, u32[]{:S(2)}) copy-start(bf16[64,64,128]{2,1,0:T(8,128)(2,1)S(1)} %get-tuple-element.5.res_v) | copy-start | bytes 3145732

commit v3 on v2

--- a/solution.py
+++ b/solution.py
@@ -31,6 +31,15 @@
     me = lax.axis_index("gx")
     col = lax.axis_index("gy")
 
+    pitch = y_points + 2 * PAD
+
+    def line(x, low=0, size=y_points):
+        start = pl.multiple_of((1 + x) * pitch, 8) + PAD
+        return pl.ds(start + low, size)
+
+    def down(y):
+        return pl.ds(pitch + PAD + y, x_points, stride=pitch)
+
     small = [
         pltpu.make_async_copy(kerr, kerr_v, small_sems.at[0]),
         pltpu.make_async_copy(wave, wave_v, small_sems.at[1]),
@@ -88,7 +97,7 @@
 
     for c in small:
         c.wait()
-    coeff = jnp.transpose(jnp.concatenate([kerr_v[...], wave_v[...]], axis=0))
+    coeff = jnp.transpose(jnp.concatenate([kerr_v[...], wave_v[...] - 4.0], axis=0))
     own = map_v[...]
     own_t = jnp.transpose(own)
     for i, m in enumerate((own, own_t)):
@@ -130,8 +139,6 @@
         run(0, me, lambda p: op_copy(1, me, p).start())
 
     def leaf_row(a):
-        rows[a][0].wait()
-        rows[a][1].wait()
         for i in range(q):
             x = a * q + i
             k = jnp.broadcast_to(coeff[:, x : x + 1], (y_points, columns))
@@ -141,10 +148,14 @@
             for b in range(leaves_y):
                 leaf_src[a, b, i * q : (i + 1) * q, :] = s[b * q : (b + 1) * q]
 
+    for a in order[:2]:
+        rows[a][0].wait()
+        rows[a][1].wait()
+    for c in edges:
+        c.wait()
     for i, a in enumerate((0, last)):
         if i == 0 or last > 0:
             leaf_row(a)
-        edges[i].wait()
         for b in range(leaves_y):
             face_out[1 - i, b * q : (b + 1) * q, :] = jnp.dot(
                 edge_ops[i, b], leaf_src[a, b], preferred_element_type=F32
@@ -153,25 +164,26 @@
     run(0, me, lambda p: face_copy(1, me, p).start())
 
     for a in order[2:]:
-        leaf_row(a)
+        rows[a][0].wait()
+        rows[a][1].wait()
     for a in order:
         ops[a].wait()
+    for a in order:
+        if a not in order[:2]:
+            leaf_row(a)
         for b in range(leaves_y):
             solved = jnp.dot(ops_v[a, b], leaf_src[a, b], preferred_element_type=F32)
             for i in range(q):
-                grid[1 + a * q + i, PAD + b * q : PAD + (b + 1) * q, :] = solved[i * q : (i + 1) * q]
-    for x in range(x_points):
-        wave_b[x] = jnp.broadcast_to(
-            coeff[:, x_points + x : x_points + x + 1] - 4.0, (y_points, columns)
-        )
-    zero_row = jnp.zeros((1, columns), F32)
-    for x in range(x_points):
-        grid[1 + x, PAD - 1 : PAD, :] = zero_row
-        grid[1 + x, PAD + y_points : PAD + y_points + 1, :] = zero_row
-    low_edge = jnp.concatenate([grid[1 + x, PAD : PAD + 1, :] for x in range(x_points)], axis=0)
-    high_edge = jnp.concatenate(
-        [grid[1 + x, PAD + y_points - 1 : PAD + y_points, :] for x in range(x_points)], axis=0
-    )
+                grid[line(a * q + i, b * q, q), :] = solved[i * q : (i + 1) * q]
+        for x in range(a * q, (a + 1) * q):
+            wave_b[x] = jnp.broadcast_to(
+                coeff[:, x_points + x : x_points + x + 1], (y_points, columns)
+            )
+    blank = jnp.zeros((x_points, columns), F32)
+    grid[down(-1), :] = blank
+    grid[down(y_points), :] = blank
+    low_edge = grid[down(0), :]
+    high_edge = grid[down(y_points - 1), :]
 
     def apply(packed, state):
         s = state.astype(BF16)
@@ -234,64 +246,72 @@
         halo_copy(1, col + 1).start()
 
     tip = 1.0 / x_points
-    body = pl.ds(PAD, y_points)
 
     @pl.when(me > 0)
     def _():
         face = face_in[jnp.maximum(me - 1, 0)].astype(F32)
-        z_there = apply(op_out[1], z) + grid[1, body, :]
+        z_there = apply(op_out[1], z) + grid[line(0), :]
         there = face + lift_weight * (tip * w_before + z_there)
-        grid[0, body, :] = there.astype(BF16).astype(F32)
+        grid[line(-1), :] = there.astype(BF16).astype(F32)
 
     @pl.when(me == 0)
     def _():
-        grid[0, body, :] = zeros
+        grid[line(-1), :] = zeros
 
     @pl.when(me < n_gx - 1)
     def _():
         face = face_in[jnp.minimum(me + 1, n_gx - 1)].astype(F32)
-        w_there = apply(op_out[0], w) + grid[x_points, body, :]
+        w_there = apply(op_out[0], w) + grid[line(x_points - 1), :]
         there = face + lift_weight * (w_there + tip * z_after)
-        grid[x_points + 1, body, :] = there.astype(BF16).astype(F32)
+        grid[line(x_points), :] = there.astype(BF16).astype(F32)
 
     @pl.when(me == n_gx - 1)
     def _():
-        grid[x_points + 1, body, :] = zeros
+        grid[line(x_points), :] = zeros
 
     def lift(x, carry):
         at = lax.convert_element_type(x, F32)
-        u = grid[1 + x, body, :] + (
+        u = grid[line(x), :] + (
             ((x_points - at) / x_points) * w3 + ((at + 1.0) / x_points) * z3
         )
         u = u.astype(BF16)
         upd_v[x] = u
-        grid[1 + x, body, :] = u.astype(F32)
+        grid[line(x), :] = u.astype(F32)
         return carry
 
     lax.fori_loop(0, x_points, lift, 0, unroll=4)
 
-    def finish(x, carry):
-        mid = grid[1 + x, body, :]
-        near = (grid[x, body, :] + grid[2 + x, body, :]) + (
-            grid[1 + x, pl.ds(PAD - 1, y_points), :] + grid[1 + x, pl.ds(PAD + 1, y_points), :]
-        )
-        factor = wave_b[x] + kerr_b[x] * (mid * mid)
-        value = near + (factor * mid - src_v[x].astype(F32))
-        rims[0, pl.ds(x, 1), :] = value[:1]
-        rims[1, pl.ds(x, 1), :] = value[y_points - 1 :]
-        res_v[x] = value.astype(BF16)
+    block = 4
+
+    def finish(i, carry):
+        x = i * block
+        for low in range(0, y_points, q):
+            part = slice(low, low + q)
+            lines = [grid[line(x + j, low, q), :] for j in range(-1, block + 1)]
+            for j in range(block):
+                mid = lines[j + 1]
+                near = (lines[j] + lines[j + 2]) + (
+                    grid[line(x + j, low - 1, q), :] + grid[line(x + j, low + 1, q), :]
+                )
+                factor = wave_b[x + j, part, :] + kerr_b[x + j, part, :] * (mid * mid)
+                value = near + (factor * mid - src_v[x + j, part, :].astype(F32))
+                if low == 0:
+                    rims[0, pl.ds(x + j, 1), :] = value[:1]
+                if low + q == y_points:
+                    rims[1, pl.ds(x + j, 1), :] = value[q - 1 :]
+                res_v[x + j, part, :] = value.astype(BF16)
         return carry
 
-    lax.fori_loop(0, x_points, finish, 0, unroll=4)
+    lax.fori_loop(0, x_points // block, finish, 0)
 
     row = lax.broadcasted_iota(jnp.int32, (q, columns), 0)
 
     def amend(side, low, at):
-        full = rims[side] + edge_in[side].astype(F32)
+        rims[side] = rims[side] + edge_in[side].astype(F32)
         for x in range(x_points):
             tile = res_v[x, low : low + q, :].astype(F32)
-            new = jnp.where(row == at, full[x : x + 1], tile)
-            res_v[x, low : low + q, :] = new.astype(BF16)
+            full = jnp.broadcast_to(rims[side, x : x + 1, :], (q, columns))
+            res_v[x, low : low + q, :] = jnp.where(row == at, full, tile).astype(BF16)
 
     @pl.when(col > 0)
     def _():
@@ -321,10 +341,13 @@
 
 
 def store(upd_v, res_v, updated, residual, sems):
-    copies = [
-        pltpu.make_async_copy(upd_v, updated, sems.at[0]),
-        pltpu.make_async_copy(res_v, residual, sems.at[1]),
-    ]
+    pieces = sems.shape[1]
+    rows = upd_v.shape[0] // pieces
+    copies = []
+    for i in range(pieces):
+        span = pl.ds(i * rows, rows)
+        copies.append(pltpu.make_async_copy(upd_v.at[span], updated.at[span], sems.at[0, i]))
+        copies.append(pltpu.make_async_copy(res_v.at[span], residual.at[span], sems.at[1, i]))
     for c in copies:
         c.start()
     for c in copies:
@@ -357,7 +380,7 @@
             pltpu.VMEM(leaf_ops.shape, BF16),
             pltpu.VMEM((2, leaves_y, q, leaf_pts), BF16),
             pltpu.VMEM((leaves_x, leaves_y, leaf_pts, columns), BF16),
-            pltpu.VMEM((x_points + 2, y_points + 2 * PAD, columns), F32),
+            pltpu.VMEM(((x_points + 2) * (y_points + 2 * PAD), columns), F32),
             pltpu.VMEM(grid_shape, F32),
             pltpu.VMEM(grid_shape, F32),
             pltpu.VMEM((2, x_points, columns), F32),
@@ -389,9 +412,10 @@
     return pl.pallas_call(
         store,
         out_shape=[pltpu.HBM(grid_shape, BF16)] * 2,
-        in_specs=[in_vmem] * 2,
+        in_specs=[pl.BlockSpec(memory_space=pl.ANY)] * 2,
         out_specs=[in_hbm] * 2,
-        scratch_shapes=[dma((2,))],
+        scratch_shapes=[dma((2, leaves_x))],
+        compiler_params=pltpu.CompilerParams(vmem_limit_bytes=1024 * 1024),
         cost_estimate=pl.CostEstimate(flops=0, bytes_accessed=4 << 20, transcendentals=0),
         name="store_results",
     )(*results)

time: 18.5 us -> 14.8 us (0.80)
  local copies, waits for them, and re-layouts: 1.98 us -> 0 us
  Pallas kernels: 15.7 us -> 14 us
    unnamed x4 -> x0, local copies, waits for them, and re-layouts: 1.98 us -> none
    pallas_call x1, Pallas kernels: 2.87 us -> 1.38 us  [per_device(): pl.pallas_call(store, out_shape=[pltpu.HBM(grid_shape, BF16)] * 2, in_spe...]
where the time goes in v3:
time: 14.8 us; the launch traced here: 14.7 us
  Pallas kernels  14 us (95%)
  between operations  0.64 us (4%)
    pallas_call x1, Pallas kernels, per_device(): pl.pallas_call(functools.partial(kernel, n_gx, n_gy), out_shape=[pltpu.VM...  12.7 us
    pallas_call x1, Pallas kernels, per_device(): pl.pallas_call(store, out_shape=[pltpu.HBM(grid_shape, BF16)] * 2, in_spe...  1.38 us

profile of v3, /device:TPU:1, one launch (start us, length us, event | category | flops | bytes accessed | tf_op | source)
XLA Modules:
  0.0 14.7 jit_solution(15131922966090507136)
XLA Ops:
  0.6 12.7 %kerr_step.1 = (bf16[64,64,128]{2,1,0:T(8,128)(2,1)S(1)}, bf16[64,64,128]{2,1,0:T(8,128)(2,1)S(1)}) custom-call(bf16[64,64,128]{2,1,0:T(8,128)(2,1)} %source.1, bf16[64,64,128]{2,1,0:T(8,128)(2,1)} %field.1, f32[64,64]{1,0:T(8,128)} %kerr.1, f32[64,64]{1,0:T(8,128)} %wave.1, bf16[4,4,256,256]{3,2,1,0:T(8,128)(2,1)} %leaf_ops.1, f32[1,64,64]{2,1,0:T(8,128)} %transfer_ops.1), custom_call_target="tpu_custom_call" | custom-call | flops 268435456 | bytes 6291456 | tf_op jit(solution)/shard_map/kerr_step/pallas_call | solution.py:369
  13.3 1.4 %store_results.1 = (bf16[64,64,128]{2,1,0:T(8,128)(2,1)}, bf16[64,64,128]{2,1,0:T(8,128)(2,1)}) custom-call(bf16[64,64,128]{2,1,0:T(8,128)(2,1)S(1)} %get-tuple-element.4.upd_v, bf16[64,64,128]{2,1,0:T(8,128)(2,1)S(1)} %get-tuple-element.5.res_v), custom_call_target="tpu_custom_call" | custom-call | bytes 4194304 | tf_op jit(solution)/shard_map/store_results/pallas_call | solution.py:412

commit v4 on v3

--- a/solution.py
+++ b/solution.py
@@ -17,9 +17,9 @@
 def kernel(
     n_gx, n_gy,
     source, field, kerr, wave, leaf_ops, transfer_ops,
-    upd_v, res_v,
+    upd_v, res_v, rims,
     src_v, fld_v, kerr_v, wave_v, map_v, ops_v, edge_ops, leaf_src, grid, kerr_b, wave_b,
-    rims, face_out, face_in, op_out, op_in, edge_out, edge_in,
+    face_out, face_in, op_out, op_in, edge_out, edge_in,
     row_sems, small_sems, ops_sems, edge_sems,
     face_send, face_recv, op_send, op_recv, halo_send, halo_recv,
 ):
@@ -168,17 +168,16 @@
         rows[a][1].wait()
     for a in order:
         ops[a].wait()
+    def solve(a, b):
+        solved = jnp.dot(ops_v[a, b], leaf_src[a, b], preferred_element_type=F32)
+        for i in range(q):
+            grid[line(a * q + i, b * q, q), :] = solved[i * q : (i + 1) * q]
+
     for a in order:
         if a not in order[:2]:
             leaf_row(a)
-        for b in range(leaves_y):
-            solved = jnp.dot(ops_v[a, b], leaf_src[a, b], preferred_element_type=F32)
-            for i in range(q):
-                grid[line(a * q + i, b * q, q), :] = solved[i * q : (i + 1) * q]
-        for x in range(a * q, (a + 1) * q):
-            wave_b[x] = jnp.broadcast_to(
-                coeff[:, x_points + x : x_points + x + 1], (y_points, columns)
-            )
+        for b in sorted({0, leaves_y - 1}):
+            solve(a, b)
     blank = jnp.zeros((x_points, columns), F32)
     grid[down(-1), :] = blank
     grid[down(y_points), :] = blank
@@ -245,6 +244,14 @@
     def _():
         halo_copy(1, col + 1).start()
 
+    for a in order:
+        for b in range(1, leaves_y - 1):
+            solve(a, b)
+        for x in range(a * q, (a + 1) * q):
+            wave_b[x] = jnp.broadcast_to(
+                coeff[:, x_points + x : x_points + x + 1], (y_points, columns)
+            )
+
     tip = 1.0 / x_points
 
     @pl.when(me > 0)
@@ -279,7 +286,7 @@
         grid[line(x), :] = u.astype(F32)
         return carry
 
-    lax.fori_loop(0, x_points, lift, 0, unroll=4)
+    lax.fori_loop(0, x_points, lift, 0, unroll=8)
 
     block = 4
 
@@ -302,54 +309,59 @@
                 res_v[x + j, part, :] = value.astype(BF16)
         return carry
 
-    lax.fori_loop(0, x_points // block, finish, 0)
-
+    lax.fori_loop(0, x_points // block, finish, 0, unroll=2)
+
+    @pl.when(col > 0)
+    def _():
+        halo_copy(1, col - 1).wait_recv()
+        rims[0] = rims[0] + edge_in[0].astype(F32)
+
+    @pl.when(col < n_gy - 1)
+    def _():
+        halo_copy(0, col + 1).wait_recv()
+        rims[1] = rims[1] + edge_in[1].astype(F32)
+
+    run(me + 1, n_gx, lambda p: face_copy(0, me, p).wait_send())
+    run(0, me, lambda p: face_copy(1, me, p).wait_send())
+
+    @pl.when(inner)
+    def _():
+        run(me + 1, n_gx, lambda p: op_copy(0, me, p).wait_send())
+        run(0, me, lambda p: op_copy(1, me, p).wait_send())
+
+    @pl.when(col > 0)
+    def _():
+        halo_copy(0, col - 1).wait_send()
+
+    @pl.when(col < n_gy - 1)
+    def _():
+        halo_copy(1, col + 1).wait_send()
+
+
+def store(pieces, upd_v, res_v, rims, updated, residual, sides, sems):
+    x_points, y_points, columns = upd_v.shape
+    q = sides.shape[2]
+    rows = x_points // pieces
+    inner = pl.ds(q, y_points - 2 * q)
+    copies = []
+
+    def send(src, dst):
+        copies.append(pltpu.make_async_copy(src, dst, sems.at[len(copies)]))
+        copies[-1].start()
+
+    for i in range(pieces):
+        span = pl.ds(i * rows, rows)
+        send(upd_v.at[span], updated.at[span])
+    for i in range(pieces):
+        span = pl.ds(i * rows, rows)
+        send(res_v.at[span, inner, :], residual.at[span, inner, :])
     row = lax.broadcasted_iota(jnp.int32, (q, columns), 0)
-
-    def amend(side, low, at):
-        rims[side] = rims[side] + edge_in[side].astype(F32)
+    for side, low, at in ((0, 0, 0), (1, y_points - q, q - 1)):
         for x in range(x_points):
             tile = res_v[x, low : low + q, :].astype(F32)
             full = jnp.broadcast_to(rims[side, x : x + 1, :], (q, columns))
-            res_v[x, low : low + q, :] = jnp.where(row == at, full, tile).astype(BF16)
-
-    @pl.when(col > 0)
-    def _():
-        halo_copy(1, col - 1).wait_recv()
-        amend(0, 0, 0)
-
-    @pl.when(col < n_gy - 1)
-    def _():
-        halo_copy(0, col + 1).wait_recv()
-        amend(1, y_points - q, q - 1)
-
-    run(me + 1, n_gx, lambda p: face_copy(0, me, p).wait_send())
-    run(0, me, lambda p: face_copy(1, me, p).wait_send())
-
-    @pl.when(inner)
-    def _():
-        run(me + 1, n_gx, lambda p: op_copy(0, me, p).wait_send())
-        run(0, me, lambda p: op_copy(1, me, p).wait_send())
-
-    @pl.when(col > 0)
-    def _():
-        halo_copy(0, col - 1).wait_send()
-
-    @pl.when(col < n_gy - 1)
-    def _():
-        halo_copy(1, col + 1).wait_send()
-
-
-def store(upd_v, res_v, updated, residual, sems):
-    pieces = sems.shape[1]
-    rows = upd_v.shape[0] // pieces
-    copies = []
-    for i in range(pieces):
-        span = pl.ds(i * rows, rows)
-        copies.append(pltpu.make_async_copy(upd_v.at[span], updated.at[span], sems.at[0, i]))
-        copies.append(pltpu.make_async_copy(res_v.at[span], residual.at[span], sems.at[1, i]))
-    for c in copies:
-        c.start()
+            sides[side, x] = jnp.where(row == at, full, tile).astype(BF16)
+        send(sides.at[side], residual.at[:, pl.ds(low, q), :])
     for c in copies:
         c.wait()
 
@@ -368,9 +380,13 @@
     ]
     results = pl.pallas_call(
         functools.partial(kernel, n_gx, n_gy),
-        out_shape=[pltpu.VMEM(grid_shape, BF16)] * 2,
+        out_shape=[
+            pltpu.VMEM(grid_shape, BF16),
+            pltpu.VMEM(grid_shape, BF16),
+            pltpu.VMEM((2, x_points, columns), F32),
+        ],
         in_specs=[in_hbm] * 6,
-        out_specs=[in_vmem] * 2,
+        out_specs=[in_vmem] * 3,
         scratch_shapes=[
             pltpu.VMEM(grid_shape, BF16),
             pltpu.VMEM(grid_shape, BF16),
@@ -383,7 +399,6 @@
             pltpu.VMEM(((x_points + 2) * (y_points + 2 * PAD), columns), F32),
             pltpu.VMEM(grid_shape, F32),
             pltpu.VMEM(grid_shape, F32),
-            pltpu.VMEM((2, x_points, columns), F32),
             pltpu.VMEM((2, y_points, columns), BF16),
             pltpu.VMEM((n_gx, y_points, columns), BF16),
             pltpu.VMEM((2, y_points // 2, 2 * y_points), BF16),
@@ -410,12 +425,15 @@
         name="kerr_step",
     )(*operands)
     return pl.pallas_call(
-        store,
+        functools.partial(store, leaves_x),
         out_shape=[pltpu.HBM(grid_shape, BF16)] * 2,
-        in_specs=[pl.BlockSpec(memory_space=pl.ANY)] * 2,
+        in_specs=[in_vmem] * 3,
         out_specs=[in_hbm] * 2,
-        scratch_shapes=[dma((2, leaves_x))],
-        compiler_params=pltpu.CompilerParams(vmem_limit_bytes=1024 * 1024),
+        scratch_shapes=[
+            pltpu.VMEM((2, x_points, q, columns), BF16),
+            dma((2 * leaves_x + 2,)),
+        ],
+        compiler_params=pltpu.CompilerParams(vmem_limit_bytes=2 * 1024 * 1024),
         cost_estimate=pl.CostEstimate(flops=0, bytes_accessed=4 << 20, transcendentals=0),
         name="store_results",
     )(*results)

time: 14.8 us -> 14.8 us (level)
  no operation moved by 1% of the time
where the time goes in v4:
time: 14.8 us; the launch traced here: 14.6 us
  Pallas kernels  14 us (95%)
  between operations  0.64 us (4%)
    pallas_call x1, Pallas kernels, per_device(): pl.pallas_call(functools.partial(kernel, n_gx, n_gy), out_shape=[pltpu.VM...  12.6 us
    pallas_call x1, Pallas kernels, per_device(): pl.pallas_call(functools.partial(store, leaves_x), out_shape=[pltpu.HBM(g...  1.4 us

profile of v4, /device:TPU:1, one launch (start us, length us, event | category | flops | bytes accessed | tf_op | source)
XLA Modules:
  0.0 14.6 jit_solution(3269325002238677333)
XLA Ops:
  0.6 12.6 %kerr_step.1 = (bf16[64,64,128]{2,1,0:T(8,128)(2,1)S(1)}, bf16[64,64,128]{2,1,0:T(8,128)(2,1)S(1)}, f32[2,64,128]{2,1,0:T(8,128)S(1)}) custom-call(bf16[64,64,128]{2,1,0:T(8,128)(2,1)} %source.1, bf16[64,64,128]{2,1,0:T(8,128)(2,1)} %field.1, f32[64,64]{1,0:T(8,128)} %kerr.1, f32[64,64]{1,0:T(8,128)} %wave.1, bf16[4,4,256,256]{3,2,1,0:T(8,128)(2,1)} %leaf_ops.1, ...), custom_call_target="tpu_custom_call" | custom-call | flops 268435456 | bytes 6291456 | tf_op jit(solution)/shard_map/kerr_step/pallas_call | solution.py:381
  13.2 1.4 %store_results.1 = (bf16[64,64,128]{2,1,0:T(8,128)(2,1)}, bf16[64,64,128]{2,1,0:T(8,128)(2,1)}) custom-call(bf16[64,64,128]{2,1,0:T(8,128)(2,1)S(1)} %get-tuple-element.5.upd_v, bf16[64,64,128]{2,1,0:T(8,128)(2,1)S(1)} %get-tuple-element.6.res_v, f32[2,64,128]{2,1,0:T(8,128)S(1)} %get-tuple-element.7.rims), custom_call_target="tpu_custom_call" | custom-call | bytes 4194304 | tf_op jit(solution)/shard_map/store_results/pallas_call | solution.py:427

commit v5 on v4

--- a/solution.py
+++ b/solution.py
@@ -40,6 +40,27 @@
     def down(y):
         return pl.ds(pitch + PAD + y, x_points, stride=pitch)
 
+    barrier = pltpu.get_barrier_semaphore()
+
+    def greet(p, carry):
+        @pl.when(p != me)
+        def _():
+            pl.semaphore_signal(barrier, inc=1, device_id={"gx": p}, device_id_type=MESH)
+
+        return carry
+
+    @pl.when(col > 0)
+    def _():
+        pl.semaphore_signal(barrier, inc=1, device_id={"gy": col - 1}, device_id_type=MESH)
+
+    @pl.when(col < n_gy - 1)
+    def _():
+        pl.semaphore_signal(barrier, inc=1, device_id={"gy": col + 1}, device_id_type=MESH)
+
+    partners = (n_gx - 1) + jnp.where(col > 0, 1, 0) + jnp.where(col < n_gy - 1, 1, 0)
+
+    lax.fori_loop(0, n_gx, greet, 0)
+
     small = [
         pltpu.make_async_copy(kerr, kerr_v, small_sems.at[0]),
         pltpu.make_async_copy(wave, wave_v, small_sems.at[1]),
@@ -74,27 +95,6 @@
     for a in order:
         ops[a].start()
 
-    barrier = pltpu.get_barrier_semaphore()
-
-    def greet(p, carry):
-        @pl.when(p != me)
-        def _():
-            pl.semaphore_signal(barrier, inc=1, device_id={"gx": p}, device_id_type=MESH)
-
-        return carry
-
-    lax.fori_loop(0, n_gx, greet, 0)
-
-    @pl.when(col > 0)
-    def _():
-        pl.semaphore_signal(barrier, inc=1, device_id={"gy": col - 1}, device_id_type=MESH)
-
-    @pl.when(col < n_gy - 1)
-    def _():
-        pl.semaphore_signal(barrier, inc=1, device_id={"gy": col + 1}, device_id_type=MESH)
-
-    partners = (n_gx - 1) + jnp.where(col > 0, 1, 0) + jnp.where(col < n_gy - 1, 1, 0)
-
     for c in small:
         c.wait()
     coeff = jnp.transpose(jnp.concatenate([kerr_v[...], wave_v[...] - 4.0], axis=0))
@@ -131,13 +131,6 @@
         lax.fori_loop(low, high, step, 0)
 
     inner = jnp.logical_and(me > 0, me < n_gx - 1)
-    pl.semaphore_wait(barrier, partners)
-
-    @pl.when(inner)
-    def _():
-        run(me + 1, n_gx, lambda p: op_copy(0, me, p).start())
-        run(0, me, lambda p: op_copy(1, me, p).start())
-
     def leaf_row(a):
         for i in range(q):
             x = a * q + i
@@ -160,8 +153,14 @@
             face_out[1 - i, b * q : (b + 1) * q, :] = jnp.dot(
                 edge_ops[i, b], leaf_src[a, b], preferred_element_type=F32
             ).astype(BF16)
+    pl.semaphore_wait(barrier, partners)
     run(me + 1, n_gx, lambda p: face_copy(0, me, p).start())
     run(0, me, lambda p: face_copy(1, me, p).start())
+
+    @pl.when(inner)
+    def _():
+        run(me + 1, n_gx, lambda p: op_copy(0, me, p).start())
+        run(0, me, lambda p: op_copy(1, me, p).start())
 
     for a in order[2:]:
         rows[a][0].wait()
@@ -184,6 +183,15 @@
     low_edge = grid[down(0), :]
     high_edge = grid[down(y_points - 1), :]
 
+    def inner_leaves():
+        for a in order:
+            for b in range(1, leaves_y - 1):
+                solve(a, b)
+            for x in range(a * q, (a + 1) * q):
+                wave_b[x] = jnp.broadcast_to(
+                    coeff[:, x_points + x : x_points + x + 1], (y_points, columns)
+                )
+
     def apply(packed, state):
         s = state.astype(BF16)
         z = jnp.zeros_like(s)
@@ -214,8 +222,39 @@
 
         return lax.fori_loop(1, count, hop, (zeros, state))
 
-    w_before, w = chain(0, me, 1)
-    z_after, z = chain(n_gx - 1, n_gx - 1 - me, -1)
+    def straight():
+        def wait(s):
+            face_copy(0, s, s).wait_recv()
+
+            @pl.when(jnp.logical_and(s > 0, s < n_gx - 1))
+            def _():
+                op_copy(0, s, s).wait_recv()
+
+        run(0, me, wait)
+        run(me + 1, n_gx, wait)
+        states = []
+        for steps, before in (
+            (range(n_gx - 1), lambda s: s < me),
+            (range(n_gx - 1, 0, -1), lambda s: s > me),
+        ):
+            prev, now = zeros, zeros
+            for s in steps:
+                nxt = face_in[s].astype(F32)
+                if s != steps[0]:
+                    nxt = nxt + apply(op_in[s], now)
+                take = before(s)
+                prev, now = jnp.where(take, now, prev), jnp.where(take, nxt, now)
+            states += [prev, now]
+        return states
+
+    if n_gx <= 8:
+        w_before, w, z_after, z = straight()
+    else:
+        w_before, w = chain(0, me, 1)
+        z_after, z = chain(n_gx - 1, n_gx - 1 - me, -1)
+    z_there = apply(op_out[1], z) + face_out[1].astype(F32)
+    w_there = apply(op_out[0], w) + face_out[0].astype(F32)
+    inner_leaves()
     w3, z3 = lift_weight * w, lift_weight * z
 
     position = lax.broadcasted_iota(jnp.int32, (x_points, columns), 0).astype(F32)
@@ -244,37 +283,14 @@
     def _():
         halo_copy(1, col + 1).start()
 
-    for a in order:
-        for b in range(1, leaves_y - 1):
-            solve(a, b)
-        for x in range(a * q, (a + 1) * q):
-            wave_b[x] = jnp.broadcast_to(
-                coeff[:, x_points + x : x_points + x + 1], (y_points, columns)
-            )
-
     tip = 1.0 / x_points
 
-    @pl.when(me > 0)
-    def _():
-        face = face_in[jnp.maximum(me - 1, 0)].astype(F32)
-        z_there = apply(op_out[1], z) + grid[line(0), :]
-        there = face + lift_weight * (tip * w_before + z_there)
-        grid[line(-1), :] = there.astype(BF16).astype(F32)
-
-    @pl.when(me == 0)
-    def _():
-        grid[line(-1), :] = zeros
-
-    @pl.when(me < n_gx - 1)
-    def _():
-        face = face_in[jnp.minimum(me + 1, n_gx - 1)].astype(F32)
-        w_there = apply(op_out[0], w) + grid[line(x_points - 1), :]
-        there = face + lift_weight * (w_there + tip * z_after)
-        grid[line(x_points), :] = there.astype(BF16).astype(F32)
-
-    @pl.when(me == n_gx - 1)
-    def _():
-        grid[line(x_points), :] = zeros
+    face = face_in[jnp.maximum(me - 1, 0)].astype(F32)
+    there = face + lift_weight * (tip * w_before + z_there)
+    grid[line(-1), :] = jnp.where(me > 0, there.astype(BF16).astype(F32), zeros)
+    face = face_in[jnp.minimum(me + 1, n_gx - 1)].astype(F32)
+    there = face + lift_weight * (w_there + tip * z_after)
+    grid[line(x_points), :] = jnp.where(me < n_gx - 1, there.astype(BF16).astype(F32), zeros)
 
     def lift(x, carry):
         at = lax.convert_element_type(x, F32)

time: 14.8 us -> 15.3 us (1.034)
  Pallas kernels: 14 us -> 14.5 us
    pallas_call x1, Pallas kernels: 12.6 us -> 13.1 us  [per_device(): pl.pallas_call(functools.partial(kernel, n_gx, n_gy), out_shape=[pltpu.VM...]
where the time goes in v5:
time: 15.3 us; the launch traced here: 15.2 us
  Pallas kernels  14.5 us (95%)
  between operations  0.64 us (4%)
    pallas_call x1, Pallas kernels, per_device(): pl.pallas_call(functools.partial(kernel, n_gx, n_gy), out_shape=[pltpu.VM...  13.1 us
    pallas_call x1, Pallas kernels, per_device(): pl.pallas_call(functools.partial(store, leaves_x), out_shape=[pltpu.HBM(g...  1.4 us

profile of v5, /device:TPU:1, one launch (start us, length us, event | category | flops | bytes accessed | tf_op | source)
XLA Modules:
  0.0 15.2 jit_solution(10378537238591750531)
XLA Ops:
  0.6 13.1 %kerr_step.1 = (bf16[64,64,128]{2,1,0:T(8,128)(2,1)S(1)}, bf16[64,64,128]{2,1,0:T(8,128)(2,1)S(1)}, f32[2,64,128]{2,1,0:T(8,128)S(1)}) custom-call(bf16[64,64,128]{2,1,0:T(8,128)(2,1)} %source.1, bf16[64,64,128]{2,1,0:T(8,128)(2,1)} %field.1, f32[64,64]{1,0:T(8,128)} %kerr.1, f32[64,64]{1,0:T(8,128)} %wave.1, bf16[4,4,256,256]{3,2,1,0:T(8,128)(2,1)} %leaf_ops.1, ...), custom_call_target="tpu_custom_call" | custom-call | flops 268435456 | bytes 6291456 | tf_op jit(solution)/shard_map/kerr_step/pallas_call | solution.py:397
  13.8 1.4 %store_results.1 = (bf16[64,64,128]{2,1,0:T(8,128)(2,1)}, bf16[64,64,128]{2,1,0:T(8,128)(2,1)}) custom-call(bf16[64,64,128]{2,1,0:T(8,128)(2,1)S(1)} %get-tuple-element.5.upd_v, bf16[64,64,128]{2,1,0:T(8,128)(2,1)S(1)} %get-tuple-element.6.res_v, f32[2,64,128]{2,1,0:T(8,128)S(1)} %get-tuple-element.7.rims), custom_call_target="tpu_custom_call" | custom-call | bytes 4194304 | tf_op jit(solution)/shard_map/store_results/pallas_call | solution.py:443

commit v6 on v5

--- a/solution.py
+++ b/solution.py
@@ -40,27 +40,6 @@
     def down(y):
         return pl.ds(pitch + PAD + y, x_points, stride=pitch)
 
-    barrier = pltpu.get_barrier_semaphore()
-
-    def greet(p, carry):
-        @pl.when(p != me)
-        def _():
-            pl.semaphore_signal(barrier, inc=1, device_id={"gx": p}, device_id_type=MESH)
-
-        return carry
-
-    @pl.when(col > 0)
-    def _():
-        pl.semaphore_signal(barrier, inc=1, device_id={"gy": col - 1}, device_id_type=MESH)
-
-    @pl.when(col < n_gy - 1)
-    def _():
-        pl.semaphore_signal(barrier, inc=1, device_id={"gy": col + 1}, device_id_type=MESH)
-
-    partners = (n_gx - 1) + jnp.where(col > 0, 1, 0) + jnp.where(col < n_gy - 1, 1, 0)
-
-    lax.fori_loop(0, n_gx, greet, 0)
-
     small = [
         pltpu.make_async_copy(kerr, kerr_v, small_sems.at[0]),
         pltpu.make_async_copy(wave, wave_v, small_sems.at[1]),
@@ -89,19 +68,36 @@
         rows[a][1].start()
     for c in edges:
         c.start()
+    barrier = pltpu.get_barrier_semaphore()
+
+    def greet(p, carry):
+        @pl.when(p != me)
+        def _():
+            pl.semaphore_signal(barrier, inc=1, device_id={"gx": p}, device_id_type=MESH)
+
+        return carry
+
+    @pl.when(col > 0)
+    def _():
+        pl.semaphore_signal(barrier, inc=1, device_id={"gy": col - 1}, device_id_type=MESH)
+
+    @pl.when(col < n_gy - 1)
+    def _():
+        pl.semaphore_signal(barrier, inc=1, device_id={"gy": col + 1}, device_id_type=MESH)
+
+    partners = (n_gx - 1) + jnp.where(col > 0, 1, 0) + jnp.where(col < n_gy - 1, 1, 0)
+
+    lax.fori_loop(0, n_gx, greet, 0)
+
     for a in order[2:]:
         rows[a][0].start()
         rows[a][1].start()
     for a in order:
         ops[a].start()
 
-    for c in small:
-        c.wait()
+    small[0].wait()
+    small[1].wait()
     coeff = jnp.transpose(jnp.concatenate([kerr_v[...], wave_v[...] - 4.0], axis=0))
-    own = map_v[...]
-    own_t = jnp.transpose(own)
-    for i, m in enumerate((own, own_t)):
-        op_out[i] = jnp.concatenate([m[:half], m[half:]], axis=1).astype(BF16)
 
     def face_copy(side, slot, p):
         return pltpu.make_async_remote_copy(
@@ -141,21 +137,27 @@
             for b in range(leaves_y):
                 leaf_src[a, b, i * q : (i + 1) * q, :] = s[b * q : (b + 1) * q]
 
-    for a in order[:2]:
-        rows[a][0].wait()
-        rows[a][1].wait()
-    for c in edges:
-        c.wait()
     for i, a in enumerate((0, last)):
         if i == 0 or last > 0:
+            rows[a][0].wait()
+            rows[a][1].wait()
             leaf_row(a)
+        edges[i].wait()
         for b in range(leaves_y):
             face_out[1 - i, b * q : (b + 1) * q, :] = jnp.dot(
                 edge_ops[i, b], leaf_src[a, b], preferred_element_type=F32
             ).astype(BF16)
-    pl.semaphore_wait(barrier, partners)
-    run(me + 1, n_gx, lambda p: face_copy(0, me, p).start())
-    run(0, me, lambda p: face_copy(1, me, p).start())
+        if i == 0:
+            pl.semaphore_wait(barrier, partners)
+            run(0, me, lambda p: face_copy(1, me, p).start())
+        else:
+            run(me + 1, n_gx, lambda p: face_copy(0, me, p).start())
+
+    small[2].wait()
+    own = map_v[...]
+    own_t = jnp.transpose(own)
+    for i, m in enumerate((own, own_t)):
+        op_out[i] = jnp.concatenate([m[:half], m[half:]], axis=1).astype(BF16)
 
     @pl.when(inner)
     def _():
@@ -183,14 +185,19 @@
     low_edge = grid[down(0), :]
     high_edge = grid[down(y_points - 1), :]
 
-    def inner_leaves():
-        for a in order:
+    def inner_leaves(part):
+        for a in part:
             for b in range(1, leaves_y - 1):
                 solve(a, b)
+
+    def wave_rows(part):
+        for a in part:
             for x in range(a * q, (a + 1) * q):
                 wave_b[x] = jnp.broadcast_to(
                     coeff[:, x_points + x : x_points + x + 1], (y_points, columns)
                 )
+
+    inner_leaves(order[:2])
 
     def apply(packed, state):
         s = state.astype(BF16)
@@ -254,7 +261,7 @@
         z_after, z = chain(n_gx - 1, n_gx - 1 - me, -1)
     z_there = apply(op_out[1], z) + face_out[1].astype(F32)
     w_there = apply(op_out[0], w) + face_out[0].astype(F32)
-    inner_leaves()
+    wave_rows(order[:2])
     w3, z3 = lift_weight * w, lift_weight * z
 
     position = lax.broadcasted_iota(jnp.int32, (x_points, columns), 0).astype(F32)
@@ -282,6 +289,9 @@
     @pl.when(col < n_gy - 1)
     def _():
         halo_copy(1, col + 1).start()
+
+    inner_leaves(order[2:])
+    wave_rows(order[2:])
 
     tip = 1.0 / x_points
 

time: 15.3 us -> 13.7 us (0.90)
  Pallas kernels: 14.5 us -> 12.9 us
    pallas_call x1, Pallas kernels: 13.1 us -> 11.5 us  [per_device(): pl.pallas_call(functools.partial(kernel, n_gx, n_gy), out_shape=[pltpu.VM...]
where the time goes in v6:
time: 13.7 us; the launch traced here: 13.6 us
  Pallas kernels  12.9 us (94%)
  between operations  0.64 us (5%)
    pallas_call x1, Pallas kernels, per_device(): pl.pallas_call(functools.partial(kernel, n_gx, n_gy), out_shape=[pltpu.VM...  11.5 us
    pallas_call x1, Pallas kernels, per_device(): pl.pallas_call(functools.partial(store, leaves_x), out_shape=[pltpu.HBM(g...  1.4 us

profile of v6, /device:TPU:1, one launch (start us, length us, event | category | flops | bytes accessed | tf_op | source)
XLA Modules:
  0.0 13.6 jit_solution(8581283847350162273)
XLA Ops:
  0.6 11.5 %kerr_step.1 = (bf16[64,64,128]{2,1,0:T(8,128)(2,1)S(1)}, bf16[64,64,128]{2,1,0:T(8,128)(2,1)S(1)}, f32[2,64,128]{2,1,0:T(8,128)S(1)}) custom-call(bf16[64,64,128]{2,1,0:T(8,128)(2,1)} %source.1, bf16[64,64,128]{2,1,0:T(8,128)(2,1)} %field.1, f32[64,64]{1,0:T(8,128)} %kerr.1, f32[64,64]{1,0:T(8,128)} %wave.1, bf16[4,4,256,256]{3,2,1,0:T(8,128)(2,1)} %leaf_ops.1, ...), custom_call_target="tpu_custom_call" | custom-call | flops 268435456 | bytes 6291456 | tf_op jit(solution)/shard_map/kerr_step/pallas_call | solution.py:407
  12.2 1.4 %store_results.1 = (bf16[64,64,128]{2,1,0:T(8,128)(2,1)}, bf16[64,64,128]{2,1,0:T(8,128)(2,1)}) custom-call(bf16[64,64,128]{2,1,0:T(8,128)(2,1)S(1)} %get-tuple-element.5.upd_v, bf16[64,64,128]{2,1,0:T(8,128)(2,1)S(1)} %get-tuple-element.6.res_v, f32[2,64,128]{2,1,0:T(8,128)S(1)} %get-tuple-element.7.rims), custom_call_target="tpu_custom_call" | custom-call | bytes 4194304 | tf_op jit(solution)/shard_map/store_results/pallas_call | solution.py:453

commit v7 on v6

--- a/solution.py
+++ b/solution.py
@@ -45,8 +45,8 @@
         pltpu.make_async_copy(wave, wave_v, small_sems.at[1]),
         pltpu.make_async_copy(transfer_ops.at[0], map_v, small_sems.at[2]),
     ]
-    for c in small:
-        c.start()
+    small[0].start()
+    small[1].start()
     order = [0, last] + list(range(1, last))
     rows, edges, ops = {}, [], {}
     for a in order:
@@ -63,11 +63,10 @@
         )
     for a in order:
         ops[a] = pltpu.make_async_copy(leaf_ops.at[a], ops_v.at[a], ops_sems.at[a])
-    for a in order[:2]:
-        rows[a][0].start()
-        rows[a][1].start()
-    for c in edges:
-        c.start()
+    rows[0][0].start()
+    rows[0][1].start()
+    edges[0].start()
+
     barrier = pltpu.get_barrier_semaphore()
 
     def greet(p, carry):
@@ -89,15 +88,20 @@
 
     lax.fori_loop(0, n_gx, greet, 0)
 
+    for a in order[1:2]:
+        rows[a][0].start()
+        rows[a][1].start()
+    edges[1].start()
+    small[2].start()
+
+    small[0].wait()
+    small[1].wait()
+    coeff = jnp.transpose(jnp.concatenate([kerr_v[...], wave_v[...] - 4.0], axis=0))
     for a in order[2:]:
         rows[a][0].start()
         rows[a][1].start()
     for a in order:
         ops[a].start()
-
-    small[0].wait()
-    small[1].wait()
-    coeff = jnp.transpose(jnp.concatenate([kerr_v[...], wave_v[...] - 4.0], axis=0))
 
     def face_copy(side, slot, p):
         return pltpu.make_async_remote_copy(
@@ -259,9 +263,6 @@
     else:
         w_before, w = chain(0, me, 1)
         z_after, z = chain(n_gx - 1, n_gx - 1 - me, -1)
-    z_there = apply(op_out[1], z) + face_out[1].astype(F32)
-    w_there = apply(op_out[0], w) + face_out[0].astype(F32)
-    wave_rows(order[:2])
     w3, z3 = lift_weight * w, lift_weight * z
 
     position = lax.broadcasted_iota(jnp.int32, (x_points, columns), 0).astype(F32)
@@ -291,7 +292,9 @@
         halo_copy(1, col + 1).start()
 
     inner_leaves(order[2:])
-    wave_rows(order[2:])
+    wave_rows(order)
+    z_there = apply(op_out[1], z) + face_out[1].astype(F32)
+    w_there = apply(op_out[0], w) + face_out[0].astype(F32)
 
     tip = 1.0 / x_points
 

time: 13.7 us -> 13.7 us (level)
  no operation moved by 1% of the time
where the time goes in v7:
time: 13.7 us; the launch traced here: 13.5 us
  Pallas kernels  12.9 us (94%)
  between operations  0.64 us (5%)
    pallas_call x1, Pallas kernels, per_device(): pl.pallas_call(functools.partial(kernel, n_gx, n_gy), out_shape=[pltpu.VM...  11.5 us
    pallas_call x1, Pallas kernels, per_device(): pl.pallas_call(functools.partial(store, leaves_x), out_shape=[pltpu.HBM(g...  1.4 us

profile of v7, /device:TPU:1, one launch (start us, length us, event | category | flops | bytes accessed | tf_op | source)
XLA Modules:
  0.0 13.5 jit_solution(3095850915355375671)
XLA Ops:
  0.6 11.5 %kerr_step.1 = (bf16[64,64,128]{2,1,0:T(8,128)(2,1)S(1)}, bf16[64,64,128]{2,1,0:T(8,128)(2,1)S(1)}, f32[2,64,128]{2,1,0:T(8,128)S(1)}) custom-call(bf16[64,64,128]{2,1,0:T(8,128)(2,1)} %source.1, bf16[64,64,128]{2,1,0:T(8,128)(2,1)} %field.1, f32[64,64]{1,0:T(8,128)} %kerr.1, f32[64,64]{1,0:T(8,128)} %wave.1, bf16[4,4,256,256]{3,2,1,0:T(8,128)(2,1)} %leaf_ops.1, ...), custom_call_target="tpu_custom_call" | custom-call | flops 268435456 | bytes 6291456 | tf_op jit(solution)/shard_map/kerr_step/pallas_call | solution.py:410
  12.1 1.4 %store_results.1 = (bf16[64,64,128]{2,1,0:T(8,128)(2,1)}, bf16[64,64,128]{2,1,0:T(8,128)(2,1)}) custom-call(bf16[64,64,128]{2,1,0:T(8,128)(2,1)S(1)} %get-tuple-element.5.upd_v, bf16[64,64,128]{2,1,0:T(8,128)(2,1)S(1)} %get-tuple-element.6.res_v, f32[2,64,128]{2,1,0:T(8,128)S(1)} %get-tuple-element.7.rims), custom_call_target="tpu_custom_call" | custom-call | bytes 4194304 | tf_op jit(solution)/shard_map/store_results/pallas_call | solution.py:456

commit v8 on v7

--- a/solution.py
+++ b/solution.py
@@ -19,9 +19,10 @@
     source, field, kerr, wave, leaf_ops, transfer_ops,
     upd_v, res_v, rims,
     src_v, fld_v, kerr_v, wave_v, map_v, ops_v, edge_ops, leaf_src, grid, kerr_b, wave_b,
-    face_out, face_in, op_out, op_in, edge_out, edge_in,
+    face_out, face_in, op_out, op_in, edge_out, edge_in, face_in_2, op_in_2,
     row_sems, small_sems, ops_sems, edge_sems,
     face_send, face_recv, op_send, op_recv, halo_send, halo_recv,
+    face_send_2, face_recv_2, op_send_2, op_recv_2,
 ):
     x_points, y_points, columns = src_v.shape
     leaves_x, leaves_y, leaf_pts, _ = ops_v.shape
@@ -30,6 +31,11 @@
     last = leaves_x - 1
     me = lax.axis_index("gx")
     col = lax.axis_index("gy")
+    odd = lax.rem(col, 2)
+    low_pair = jnp.logical_and(odd == 0, col > 0)
+    high_pair = jnp.logical_and(odd == 1, col < n_gy - 1)
+    has_pair = jnp.logical_or(low_pair, high_pair)
+    pair = jnp.where(high_pair, col + 1, jnp.where(low_pair, col - 1, col))
 
     pitch = y_points + 2 * PAD
 
@@ -74,6 +80,12 @@
         def _():
             pl.semaphore_signal(barrier, inc=1, device_id={"gx": p}, device_id_type=MESH)
 
+            @pl.when(has_pair)
+            def _():
+                pl.semaphore_signal(
+                    barrier, inc=1, device_id={"gx": p, "gy": pair}, device_id_type=MESH
+                )
+
         return carry
 
     @pl.when(col > 0)
@@ -85,6 +97,7 @@
         pl.semaphore_signal(barrier, inc=1, device_id={"gy": col + 1}, device_id_type=MESH)
 
     partners = (n_gx - 1) + jnp.where(col > 0, 1, 0) + jnp.where(col < n_gy - 1, 1, 0)
+    partners = partners + jnp.where(has_pair, n_gx - 1, 0)
 
     lax.fori_loop(0, n_gx, greet, 0)
 
@@ -103,23 +116,33 @@
     for a in order:
         ops[a].start()
 
-    def face_copy(side, slot, p):
+    def face_copy(side, slot, p, other=False):
         return pltpu.make_async_remote_copy(
             src_ref=face_out.at[side],
-            dst_ref=face_in.at[slot],
-            send_sem=face_send.at[p],
-            recv_sem=face_recv.at[slot],
-            device_id={"gx": p},
+            dst_ref=(face_in_2 if other else face_in).at[slot],
+            send_sem=(face_send_2 if other else face_send).at[p],
+            recv_sem=(face_recv_2 if other else face_recv).at[slot],
+            device_id={"gx": p, "gy": pair} if other else {"gx": p},
             device_id_type=MESH,
         )
 
-    def op_copy(side, slot, p):
+    def op_copy(side, slot, p, other=False):
         return pltpu.make_async_remote_copy(
             src_ref=op_out.at[side],
-            dst_ref=op_in.at[slot],
-            send_sem=op_send.at[p],
-            recv_sem=op_recv.at[slot],
-            device_id={"gx": p},
+            dst_ref=(op_in_2 if other else op_in).at[slot],
+            send_sem=(op_send_2 if other else op_send).at[p],
+            recv_sem=(op_recv_2 if other else op_recv).at[slot],
+            device_id={"gx": p, "gy": pair} if other else {"gx": p},
+            device_id_type=MESH,
+        )
+
+    def halo_copy(side, p):
+        return pltpu.make_async_remote_copy(
+            src_ref=edge_out.at[side],
+            dst_ref=edge_in.at[1 - side],
+            send_sem=halo_send.at[side],
+            recv_sem=halo_recv.at[1 - side],
+            device_id={"gy": p},
             device_id_type=MESH,
         )
 
@@ -131,6 +154,8 @@
         lax.fori_loop(low, high, step, 0)
 
     inner = jnp.logical_and(me > 0, me < n_gx - 1)
+    low_end = jnp.where(has_pair, me, 0)
+    high_end = jnp.where(has_pair, n_gx, me + 1)
     def leaf_row(a):
         for i in range(q):
             x = a * q + i
@@ -154,8 +179,10 @@
         if i == 0:
             pl.semaphore_wait(barrier, partners)
             run(0, me, lambda p: face_copy(1, me, p).start())
+            run(0, low_end, lambda p: face_copy(1, me, p, True).start())
         else:
             run(me + 1, n_gx, lambda p: face_copy(0, me, p).start())
+            run(me + 1, high_end, lambda p: face_copy(0, me, p, True).start())
 
     small[2].wait()
     own = map_v[...]
@@ -167,6 +194,8 @@
     def _():
         run(me + 1, n_gx, lambda p: op_copy(0, me, p).start())
         run(0, me, lambda p: op_copy(1, me, p).start())
+        run(me + 1, high_end, lambda p: op_copy(0, me, p, True).start())
+        run(0, low_end, lambda p: op_copy(1, me, p, True).start())
 
     for a in order[2:]:
         rows[a][0].wait()
@@ -203,6 +232,16 @@
 
     inner_leaves(order[:2])
 
+    @pl.when(low_pair)
+    def _():
+        edge_out[0] = low_edge.astype(BF16)
+        halo_copy(0, col - 1).start()
+
+    @pl.when(high_pair)
+    def _():
+        edge_out[1] = high_edge.astype(BF16)
+        halo_copy(1, col + 1).start()
+
     def apply(packed, state):
         s = state.astype(BF16)
         z = jnp.zeros_like(s)
@@ -214,35 +253,35 @@
 
     zeros = jnp.zeros((y_points, columns), F32)
 
-    def arrived(s):
-        face_copy(0, s, s).wait_recv()
-        return face_in[s].astype(F32)
-
-    def chain(begin, count, step):
-        def first():
-            return arrived(begin)
-
-        state = lax.cond(count > 0, first, lambda: zeros)
+    def chain(begin, count, step, other):
+        faces, ops_in = (face_in_2, op_in_2) if other else (face_in, op_in)
+
+        def arrived(s):
+            face_copy(0, s, s, other).wait_recv()
+            return faces[s].astype(F32)
+
+        state = lax.cond(count > 0, lambda: arrived(begin), lambda: zeros)
 
         def hop(i, carry):
             _, now = carry
             s = begin + step * i
-            op_copy(0, s, s).wait_recv()
-            nxt = apply(op_in[s], now) + arrived(s)
-            return now, nxt
+            op_copy(0, s, s, other).wait_recv()
+            return now, apply(ops_in[s], now) + arrived(s)
 
         return lax.fori_loop(1, count, hop, (zeros, state))
 
-    def straight():
+    def straight(other):
+        faces, ops_in = (face_in_2, op_in_2) if other else (face_in, op_in)
+
         def wait(s):
-            face_copy(0, s, s).wait_recv()
+            face_copy(0, s, s, other).wait_recv()
 
             @pl.when(jnp.logical_and(s > 0, s < n_gx - 1))
             def _():
-                op_copy(0, s, s).wait_recv()
-
-        run(0, me, wait)
-        run(me + 1, n_gx, wait)
+                op_copy(0, s, s, other).wait_recv()
+
+        run(0, low_end if other else me, wait)
+        run(me + 1, high_end if other else n_gx, wait)
         states = []
         for steps, before in (
             (range(n_gx - 1), lambda s: s < me),
@@ -250,47 +289,46 @@
         ):
             prev, now = zeros, zeros
             for s in steps:
-                nxt = face_in[s].astype(F32)
+                nxt = faces[s].astype(F32)
                 if s != steps[0]:
-                    nxt = nxt + apply(op_in[s], now)
+                    nxt = nxt + apply(ops_in[s], now)
                 take = before(s)
                 prev, now = jnp.where(take, now, prev), jnp.where(take, nxt, now)
             states += [prev, now]
         return states
 
-    if n_gx <= 8:
-        w_before, w, z_after, z = straight()
-    else:
-        w_before, w = chain(0, me, 1)
-        z_after, z = chain(n_gx - 1, n_gx - 1 - me, -1)
+    def chains(other):
+        if n_gx <= 8:
+            return straight(other)
+        before, after = me, n_gx - 1 - me
+        if other:
+            before, after = jnp.where(has_pair, before, 0), jnp.where(has_pair, after, 0)
+        return (*chain(0, before, 1, other), *chain(n_gx - 1, after, -1, other))
+
+    w_before, w, z_after, z = chains(False)
     w3, z3 = lift_weight * w, lift_weight * z
 
     position = lax.broadcasted_iota(jnp.int32, (x_points, columns), 0).astype(F32)
     left_prof = (x_points - position) / x_points
     right_prof = (position + 1.0) / x_points
-    for i, (edge, y) in enumerate(((low_edge, 0), (high_edge, y_points - 1))):
-        edge_out[i] = (
-            edge + (left_prof * w3[y : y + 1, :] + right_prof * z3[y : y + 1, :])
+
+    def lifted(edge, w_side, z_side, y):
+        return (
+            edge + (left_prof * w_side[y : y + 1, :] + right_prof * z_side[y : y + 1, :])
         ).astype(BF16)
 
-    def halo_copy(side, p):
-        return pltpu.make_async_remote_copy(
-            src_ref=edge_out.at[side],
-            dst_ref=edge_in.at[1 - side],
-            send_sem=halo_send.at[side],
-            recv_sem=halo_recv.at[1 - side],
-            device_id={"gy": p},
-            device_id_type=MESH,
-        )
-
-    @pl.when(col > 0)
-    def _():
+    @pl.when(odd == 1)
+    def _():
+        edge_out[0] = lifted(low_edge, w3, z3, 0)
         halo_copy(0, col - 1).start()
 
-    @pl.when(col < n_gy - 1)
-    def _():
+    @pl.when(jnp.logical_and(odd == 0, col < n_gy - 1))
+    def _():
+        edge_out[1] = lifted(high_edge, w3, z3, y_points - 1)
         halo_copy(1, col + 1).start()
 
+    _, w_pair, _, z_pair = chains(True)
+    w_pair, z_pair = lift_weight * w_pair, lift_weight * z_pair
     inner_leaves(order[2:])
     wave_rows(order)
     z_there = apply(op_out[1], z) + face_out[1].astype(F32)
@@ -343,20 +381,28 @@
     @pl.when(col > 0)
     def _():
         halo_copy(1, col - 1).wait_recv()
-        rims[0] = rims[0] + edge_in[0].astype(F32)
+        got = edge_in[0].astype(F32)
+        full = lifted(got, w_pair, z_pair, y_points - 1).astype(F32)
+        rims[0] = rims[0] + jnp.where(low_pair, full, got)
 
     @pl.when(col < n_gy - 1)
     def _():
         halo_copy(0, col + 1).wait_recv()
-        rims[1] = rims[1] + edge_in[1].astype(F32)
+        got = edge_in[1].astype(F32)
+        full = lifted(got, w_pair, z_pair, 0).astype(F32)
+        rims[1] = rims[1] + jnp.where(high_pair, full, got)
 
     run(me + 1, n_gx, lambda p: face_copy(0, me, p).wait_send())
     run(0, me, lambda p: face_copy(1, me, p).wait_send())
+    run(me + 1, high_end, lambda p: face_copy(0, me, p, True).wait_send())
+    run(0, low_end, lambda p: face_copy(1, me, p, True).wait_send())
 
     @pl.when(inner)
     def _():
         run(me + 1, n_gx, lambda p: op_copy(0, me, p).wait_send())
         run(0, me, lambda p: op_copy(1, me, p).wait_send())
+        run(me + 1, high_end, lambda p: op_copy(0, me, p, True).wait_send())
+        run(0, low_end, lambda p: op_copy(1, me, p, True).wait_send())
 
     @pl.when(col > 0)
     def _():
@@ -434,6 +480,8 @@
             pltpu.VMEM((n_gx, y_points // 2, 2 * y_points), BF16),
             pltpu.VMEM((2, x_points, columns), BF16),
             pltpu.VMEM((2, x_points, columns), BF16),
+            pltpu.VMEM((n_gx, y_points, columns), BF16),
+            pltpu.VMEM((n_gx, y_points // 2, 2 * y_points), BF16),
             dma((2, leaves_x)),
             dma((3,)),
             dma((leaves_x,)),
@@ -444,6 +492,7 @@
             dma((n_gx,)),
             dma((2,)),
             dma((2,)),
+            *[dma((n_gx,))] * 4,
         ],
         compiler_params=pltpu.CompilerParams(
             collective_id=0, has_side_effects=True, vmem_limit_bytes=40 * 1024 * 1024

time: 13.7 us -> 14.3 us (1.044)
  Pallas kernels: 12.9 us -> 13.6 us
    pallas_call x1, Pallas kernels: 11.5 us -> 12.2 us  [per_device(): pl.pallas_call(functools.partial(kernel, n_gx, n_gy), out_shape=[pltpu.VM...]
where the time goes in v8:
time: 14.3 us; the launch traced here: 14.2 us
  Pallas kernels  13.6 us (95%)
  between operations  0.64 us (4%)
    pallas_call x1, Pallas kernels, per_device(): pl.pallas_call(functools.partial(kernel, n_gx, n_gy), out_shape=[pltpu.VM...  12.2 us
    pallas_call x1, Pallas kernels, per_device(): pl.pallas_call(functools.partial(store, leaves_x), out_shape=[pltpu.HBM(g...  1.4 us

profile of v8, /device:TPU:1, one launch (start us, length us, event | category | flops | bytes accessed | tf_op | source)
XLA Modules:
  0.0 14.2 jit_solution(5934027784147667355)
XLA Ops:
  0.6 12.2 %kerr_step.1 = (bf16[64,64,128]{2,1,0:T(8,128)(2,1)S(1)}, bf16[64,64,128]{2,1,0:T(8,128)(2,1)S(1)}, f32[2,64,128]{2,1,0:T(8,128)S(1)}) custom-call(bf16[64,64,128]{2,1,0:T(8,128)(2,1)} %source.1, bf16[64,64,128]{2,1,0:T(8,128)(2,1)} %field.1, f32[64,64]{1,0:T(8,128)} %kerr.1, f32[64,64]{1,0:T(8,128)} %wave.1, bf16[4,4,256,256]{3,2,1,0:T(8,128)(2,1)} %leaf_ops.1, ...), custom_call_target="tpu_custom_call" | custom-call | flops 268435456 | bytes 6291456 | tf_op jit(solution)/shard_map/kerr_step/pallas_call | solution.py:456
  12.8 1.4 %store_results.1 = (bf16[64,64,128]{2,1,0:T(8,128)(2,1)}, bf16[64,64,128]{2,1,0:T(8,128)(2,1)}) custom-call(bf16[64,64,128]{2,1,0:T(8,128)(2,1)S(1)} %get-tuple-element.5.upd_v, bf16[64,64,128]{2,1,0:T(8,128)(2,1)S(1)} %get-tuple-element.6.res_v, f32[2,64,128]{2,1,0:T(8,128)S(1)} %get-tuple-element.7.rims), custom_call_target="tpu_custom_call" | custom-call | bytes 4194304 | tf_op jit(solution)/shard_map/store_results/pallas_call | solution.py:505

commit v9 on v7

--- a/solution.py
+++ b/solution.py
@@ -141,6 +141,12 @@
             for b in range(leaves_y):
                 leaf_src[a, b, i * q : (i + 1) * q, :] = s[b * q : (b + 1) * q]
 
+    def pack():
+        small[2].wait()
+        own = map_v[...]
+        for i, m in enumerate((own, jnp.transpose(own))):
+            op_out[i] = jnp.concatenate([m[:half], m[half:]], axis=1).astype(BF16)
+
     for i, a in enumerate((0, last)):
         if i == 0 or last > 0:
             rows[a][0].wait()
@@ -152,21 +158,21 @@
                 edge_ops[i, b], leaf_src[a, b], preferred_element_type=F32
             ).astype(BF16)
         if i == 0:
+            pl.when(inner)(pack)
             pl.semaphore_wait(barrier, partners)
             run(0, me, lambda p: face_copy(1, me, p).start())
+
+            @pl.when(inner)
+            def _():
+                run(0, me, lambda p: op_copy(1, me, p).start())
+                run(me + 1, n_gx, lambda p: op_copy(0, me, p).start())
+
         else:
             run(me + 1, n_gx, lambda p: face_copy(0, me, p).start())
 
-    small[2].wait()
-    own = map_v[...]
-    own_t = jnp.transpose(own)
-    for i, m in enumerate((own, own_t)):
-        op_out[i] = jnp.concatenate([m[:half], m[half:]], axis=1).astype(BF16)
-
-    @pl.when(inner)
-    def _():
-        run(me + 1, n_gx, lambda p: op_copy(0, me, p).start())
-        run(0, me, lambda p: op_copy(1, me, p).start())
+    @pl.when(jnp.logical_not(inner))
+    def _():
+        pack()
 
     for a in order[2:]:
         rows[a][0].wait()

time: 13.7 us -> 13.7 us (level)
  no operation moved by 1% of the time
where the time goes in v9:
time: 13.7 us; the launch traced here: 13.5 us
  Pallas kernels  12.9 us (94%)
  between operations  0.64 us (5%)
    pallas_call x1, Pallas kernels, per_device(): pl.pallas_call(functools.partial(kernel, n_gx, n_gy), out_shape=[pltpu.VM...  11.5 us
    pallas_call x1, Pallas kernels, per_device(): pl.pallas_call(functools.partial(store, leaves_x), out_shape=[pltpu.HBM(g...  1.4 us

profile of v9, /device:TPU:1, one launch (start us, length us, event | category | flops | bytes accessed | tf_op | source)
XLA Modules:
  0.0 13.5 jit_solution(1216179896670334489)
XLA Ops:
  0.6 11.5 %kerr_step.1 = (bf16[64,64,128]{2,1,0:T(8,128)(2,1)S(1)}, bf16[64,64,128]{2,1,0:T(8,128)(2,1)S(1)}, f32[2,64,128]{2,1,0:T(8,128)S(1)}) custom-call(bf16[64,64,128]{2,1,0:T(8,128)(2,1)} %source.1, bf16[64,64,128]{2,1,0:T(8,128)(2,1)} %field.1, f32[64,64]{1,0:T(8,128)} %kerr.1, f32[64,64]{1,0:T(8,128)} %wave.1, bf16[4,4,256,256]{3,2,1,0:T(8,128)(2,1)} %leaf_ops.1, ...), custom_call_target="tpu_custom_call" | custom-call | flops 268435456 | bytes 6291456 | tf_op jit(solution)/shard_map/kerr_step/pallas_call | solution.py:416
  12.1 1.4 %store_results.1 = (bf16[64,64,128]{2,1,0:T(8,128)(2,1)}, bf16[64,64,128]{2,1,0:T(8,128)(2,1)}) custom-call(bf16[64,64,128]{2,1,0:T(8,128)(2,1)S(1)} %get-tuple-element.5.upd_v, bf16[64,64,128]{2,1,0:T(8,128)(2,1)S(1)} %get-tuple-element.6.res_v, f32[2,64,128]{2,1,0:T(8,128)S(1)} %get-tuple-element.7.rims), custom_call_target="tpu_custom_call" | custom-call | bytes 4194304 | tf_op jit(solution)/shard_map/store_results/pallas_call | solution.py:462
